TPU v7x, 512 devices: a whole 4x4x16 slice. The times are simulated.
512 devices in a mesh: epoch: 4 (over x), batch: 32 (over y, z_lo), mem: 4 (over z_hi, core).
Axes of the slice: x: 4, y: 4, z: 16 (z_hi: 2, z_lo: 8; z = z_hi * 8 + z_lo), core: 2. Of those that a mesh axis runs over, the one named last changes fastest.
Arguments:
- node_memory: bfloat16 [65536, 512], P(('batch', 'mem')), may hold values from -3 to 3
- neighbour_ids: int32 [10, 65536], P(None, ('batch', 'mem')), may hold values from 0 to 511
- neighbour_ticks: int32 [10, 65536], P(None, ('batch', 'mem')), may hold values from 0 to 999
- source_ids: int32 [4, 2, 32768], P('epoch', None, ('batch', 'mem')), may hold values from 0 to 511
- target_ids: int32 [4, 2, 32768], P('epoch', None, ('batch', 'mem')), may hold values from 0 to 511, as said below
- negative_ids: int32 [4, 2, 32768], P('epoch', None, ('batch', 'mem')), may hold values from 0 to 511
- event_ticks: int32 [4, 2, 32768], P('epoch', None, ('batch', 'mem')), may hold values from 1000 to 4999
- gru_input: bfloat16 [512, 1536], replicated, may hold values from -0.25 to 0.25
- gru_state: bfloat16 [512, 1536], replicated, may hold values from -0.25 to 0.25
- decoder_weight: bfloat16 [512, 256], replicated, may hold values from -0.25 to 0.25
Outputs:
- memory_out: bfloat16 [4, 65536, 512], P('epoch', ('batch', 'mem'))
- decoder_out: float32 [4, 512, 256], P('epoch')
- logits_out: float32 [4, 4, 32768], P('epoch', None, ('batch', 'mem'))
Inputs may be any that keep to these rules, and one draw needn't show every extreme that they name: `target_ids`: within one device's 256 events of one mini-batch the targets are distinct, and the last row of the block is among them.
All inputs are finite; a program needn't handle non-finite values.
Results may differ from a plain program's by a relative error of at most 0.0034.
Values may be sent and summed in bfloat16 or wider, within the bound.
A program may use at most 64 MiB of HBM per device.

v0:
```python
import jax
import jax.numpy as jnp
from jax import lax
from jax.sharding import PartitionSpec as P

tick_scale = 100.0
step_length = 4.0
epsilon = 1e-06


def passed_along(array, axis, by):
    length = lax.axis_size(axis)
    return lax.ppermute(array, axis, [(i, (i + by) % length) for i in range(length)])


def fresh_memory(memory_block, near_table, near_times, source, target, ticks, gru_input, gru_state):
    width = memory_block.shape[1]
    source_rows = jnp.take(memory_block, source, axis=0)
    target_rows = jnp.take(memory_block, target, axis=0)
    near_ids = jnp.take(near_table, target, axis=1)
    near_ticks = jnp.take(near_times, target, axis=1)
    decay = tick_scale / (tick_scale + (ticks[None, :] - near_ticks).astype(jnp.float32))
    summed = jnp.zeros((target.shape[0], width), jnp.float32)
    for slot in range(near_ids.shape[0]):
        near_rows = jnp.take(memory_block, near_ids[slot], axis=0)
        summed = summed + decay[slot][:, None] * near_rows.astype(jnp.float32)
    aggregate = summed / jnp.sum(decay, axis=0)[:, None]
    input_gates = jnp.dot(source_rows, gru_input, preferred_element_type=jnp.float32)
    state_gates = jnp.dot(target_rows, gru_state, preferred_element_type=jnp.float32)
    reset = jax.nn.sigmoid(input_gates[:, :width] + state_gates[:, :width])
    update = jax.nn.sigmoid(input_gates[:, width : 2 * width] + state_gates[:, width : 2 * width])
    candidate = jnp.tanh(input_gates[:, 2 * width :] + reset * state_gates[:, 2 * width :])
    fresh = ((1.0 - update) * candidate + update * target_rows.astype(jnp.float32)).astype(
        jnp.bfloat16
    )
    return (fresh, aggregate)


def link_terms(memory_block, source, target, negative, aggregate, decoder_bf):
    scale = 1.0 / jnp.sqrt(jnp.float32(decoder_bf.shape[1]))
    source_rows = jnp.take(memory_block, source, axis=0)
    target_rows = jnp.take(memory_block, target, axis=0)
    negative_rows = jnp.take(memory_block, negative, axis=0)
    target_embed = (0.5 * (target_rows.astype(jnp.float32) + aggregate)).astype(jnp.bfloat16)
    stacked = jnp.concatenate([source_rows, target_embed, negative_rows], axis=0)
    projected = jnp.dot(stacked, decoder_bf, preferred_element_type=jnp.float32)
    count = source.shape[0]
    proj_source = projected[:count]
    proj_target = projected[count : 2 * count]
    proj_negative = projected[2 * count :]
    positive = jnp.sum(proj_source * proj_target, axis=1) * scale
    negative_logit = jnp.sum(proj_source * proj_negative, axis=1) * scale
    grad_positive = -jax.nn.sigmoid(-positive) * scale
    grad_negative = jax.nn.sigmoid(negative_logit) * scale
    delta_source = (
        grad_positive[:, None] * proj_target + grad_negative[:, None] * proj_negative
    ).astype(jnp.bfloat16)
    delta_target = (grad_positive[:, None] * proj_source).astype(jnp.bfloat16)
    delta_negative = (grad_negative[:, None] * proj_source).astype(jnp.bfloat16)
    deltas = jnp.concatenate([delta_source, delta_target, delta_negative], axis=0)
    gradient = lax.dot_general(
        stacked, deltas, (((0,), (0,)), ((), ())), preferred_element_type=jnp.float32
    )
    return (positive, negative_logit, gradient)


def take_step(master, gradient):
    total = lax.psum(gradient, ("batch", "mem"))
    return master - step_length * total / jnp.sqrt(jnp.sum(total * total) + epsilon)


def on_device(
    node_memory,
    neighbour_ids,
    neighbour_ticks,
    source_ids,
    target_ids,
    negative_ids,
    event_ticks,
    gru_input,
    gru_state,
    decoder_weight,
):
    master = decoder_weight.astype(jnp.float32)
    first_fresh, first_aggregate = fresh_memory(
        node_memory,
        neighbour_ids,
        neighbour_ticks,
        source_ids[0, 0],
        target_ids[0, 0],
        event_ticks[0, 0],
        gru_input,
        gru_state,
    )
    first_positive, first_negative, first_gradient = link_terms(
        node_memory,
        source_ids[0, 0],
        target_ids[0, 0],
        negative_ids[0, 0],
        first_aggregate,
        master.astype(jnp.bfloat16),
    )
    first_memory = node_memory.at[target_ids[0, 0]].set(first_fresh)
    second_memory = passed_along(first_memory, "epoch", 1)
    master = take_step(master, first_gradient)
    second_fresh, second_aggregate = fresh_memory(
        second_memory,
        neighbour_ids,
        neighbour_ticks,
        source_ids[0, 1],
        target_ids[0, 1],
        event_ticks[0, 1],
        gru_input,
        gru_state,
    )
    final_memory = second_memory.at[target_ids[0, 1]].set(second_fresh)
    second_positive, second_negative, second_gradient = link_terms(
        second_memory,
        source_ids[0, 1],
        target_ids[0, 1],
        negative_ids[0, 1],
        second_aggregate,
        master.astype(jnp.bfloat16),
    )
    master = take_step(master, second_gradient)
    logit_rows = jnp.stack([first_positive, first_negative, second_positive, second_negative])
    return (final_memory[None], master[None], logit_rows[None])


def solution(mesh):
    in_specs = (
        P(("batch", "mem"), None),
        P(None, ("batch", "mem")),
        P(None, ("batch", "mem")),
        P("epoch", None, ("batch", "mem")),
        P("epoch", None, ("batch", "mem")),
        P("epoch", None, ("batch", "mem")),
        P("epoch", None, ("batch", "mem")),
        P(),
        P(),
        P(),
    )
    out_specs = (
        P("epoch", ("batch", "mem"), None),
        P("epoch", None, None),
        P("epoch", None, ("batch", "mem")),
    )
    return jax.shard_map(
        on_device, mesh=mesh, in_specs=in_specs, out_specs=out_specs, check_vma=False
    )
```

profile of v0, /device:TPU:1, one launch (start us, length us, event | category | flops | bytes accessed | tf_op | source)
XLA Modules:
  0.0 758.6 jit_solution(4117992784067925785)
XLA Ops:
  29.6 1.9 gather_fusion.11
  31.4 1.9 gather_fusion.10
  33.3 1.9 gather_fusion.9
  35.1 1.9 gather_fusion.8
  37.0 1.9 gather_fusion.7
  38.9 1.9 gather_fusion.6
  43.2 2.0 gather_fusion.15
  46.7 2.8 fusion.3
  52.0 3.2 fusion.70
  57.0 3.4 scatter_custom_fusion
  60.4 4.0 collective-permute-start
  67.7 319.2 %all-reduce.3.cloned.1.call-done = f32[512,256]{1,0:T(8,128)} async-done(((f32[512,256]{1,0:T(8,128)}), f32[512,256]{1,0:T(8,128)}) %all-reduce.3.cloned.1.call-update) | async-done | bytes 524304 | tf_op jit(solution)/shard_map/psum | solution.py:68
  396.6 1.9 gather_fusion.27
  398.4 1.9 gather_fusion.26
  400.3 1.9 gather_fusion.25
  402.1 1.9 gather_fusion.24
  405.9 1.9 gather_fusion.22
  407.7 1.9 gather_fusion.21
  411.4 1.9 gather_fusion.19
  413.3 2.8 fusion.7
  418.0 3.1 fusion.71
  421.1 3.4 scatter_custom_fusion.1
  425.2 321.3 %all-reduce.5.cloned.1.call-done = f32[512,256]{1,0:T(8,128)} async-done(((f32[512,256]{1,0:T(8,128)}), f32[512,256]{1,0:T(8,128)}) %all-reduce.5.cloned.1.call-update) | async-done | bytes 524304 | tf_op jit(solution)/shard_map/psum | solution.py:68
  749.0 2.0 subtract_bitcast_fusion
  (145 shorter events, 51.1 us)
Async XLA Ops:
  7.2 48.1 %copy-start = (bf16[512,1536]{1,0:T(8,128)(2,1)S(1)}, bf16[512,1536]{1,0:T(8,128)(2,1)}, u32[]{:S(2)}) copy-start(bf16[512,1536]{1,0:T(8,128)(2,1)} %param.22) | copy-start | bytes 4718596
  7.2 12.5 %copy-start.7 = (s32[10,512]{1,0:T(8,128)S(1)}, s32[10,512]{1,0:T(8,128)}, u32[]{:S(2)}) copy-start(s32[10,512]{1,0:T(8,128)} %param.16) | copy-start | bytes 61444
  7.2 11.2 %copy-start.13 = (s32[1,2,256]{2,1,0:T(2,128)S(1)}, s32[1,2,256]{2,1,0:T(2,128)}, u32[]{:S(2)}) copy-start(s32[1,2,256]{2,1,0:T(2,128)} %param.20) | copy-start | bytes 6148
  7.2 379.7 %all-reduce.3.cloned.1.call-start = ((), (), s32[]{:S(2)}) async-start(), calls=%async_computation | async-start | bytes 1048576 | tf_op jit(solution)/shard_map/psum | solution.py:68
  43.2 3.5 copy-start.10
  45.9 4.3 copy-start.2
  46.6 2.9 copy-start.3
  50.1 1.3 copy-start.8
  51.4 695.1 %all-reduce.5.cloned.1.call-start = ((), (), s32[]{:S(2)}) async-start(), calls=%async_computation.1 | async-start | bytes 1048576 | tf_op jit(solution)/shard_map/psum | solution.py:68
  57.0 7.4 copy-start.11
  57.0 7.4 copy-start.12
  60.4 328.9 %collective-permute-start = (bf16[512,512]{1,0:T(8,128)(2,1)S(1)}, bf16[512,512]{1,0:T(8,128)(2,1)S(1)}, u32[]{:S(2)}, u32[]{:S(2)}) collective-permute-start(bf16[512,512]{1,0:T(8,128)(2,1)S(1)} %scatter_custom_fusion), channel_id=1, source_target_pairs={{0,128},{128,256},{256,384},{384,0},{1,129},{129,257},{257,385},{3... | collective-permute-start | bytes 1572872 | tf_op jit(solution)/shard_map/ppermute | solution.py:13
  411.4 1.9 copy-start.9
  411.4 1.9 copy-start.14
  413.3 2.8 copy-start.1
  413.3 2.8 copy-start.4
  413.3 2.8 copy-start.6
  421.1 327.8 %copy-start.5 = (bf16[512,256]{1,0:T(8,128)(2,1)S(1)}, bf16[512,256]{1,0:T(8,128)(2,1)}, u32[]{:S(2)}) copy-start(bf16[512,256]{1,0:T(8,128)(2,1)} %param.23) | copy-start | bytes 786436
Sparse Core Ops, SparseCore 0:
  51.5 335.3 all-reduce.2
  418.1 328.3 all-reduce.4
where the time goes:
time: 759 us
  waiting for transfers between devices  641 us (84%)
  local copies, waits for them, and re-layouts  56 us (7%)
  other arithmetic  28.8 us (4%)
  between operations  16 us (2%)
  matrix products  13.1 us (2%)
    psum x2, waiting for transfers between devices, take_step(): total = lax.psum(gradient, ('batch', 'mem'))  641 us
    gather x20, local copies, waits for them, and re-layouts, fresh_memory(): near_rows = jnp.take(memory_block, near_ids[slot], axis=0)  35.9 us
  transfers between devices with their start and end apart: 3, of which 2 were waited for; matrix products, arithmetic and copies ran while one was open for 3% of the time, Pallas kernels for 0%

commit v1 on v0

--- a/solution.py
+++ b/solution.py
@@ -1,6 +1,8 @@
 import jax
 import jax.numpy as jnp
 from jax import lax
+from jax.experimental import pallas as pl
+from jax.experimental.pallas import tpu as pltpu
 from jax.sharding import PartitionSpec as P
 
 tick_scale = 100.0
@@ -64,8 +66,164 @@
     return (positive, negative_logit, gradient)
 
 
-def take_step(master, gradient):
-    total = lax.psum(gradient, ("batch", "mem"))
+MESH = pl.DeviceIdType.MESH
+near_peers = [(y, c) for y in range(4) for c in range(2) if (y, c) != (0, 0)]
+ring = 16
+
+
+def place():
+    batch, mem = lax.axis_index("batch"), lax.axis_index("mem")
+    return batch // 8, (mem // 2) * 8 + batch % 8, mem % 2
+
+
+def device_at(y, z, core):
+    return {"batch": y * 8 + z % 8, "mem": (z // 8) * 2 + core}
+
+
+def sum_kernel(
+    gradient,
+    total,
+    rounded,
+    near_in,
+    piece,
+    far_in,
+    all_parts,
+    joined,
+    near_send,
+    near_recv,
+    far_send,
+    far_recv,
+    back_send,
+    back_recv,
+    last_send,
+    last_recv,
+):
+    y, z, core = place()
+    rows = 64
+    near = [(dy * 2 + dc, (y + dy) % 4, (core + dc) % 2) for dy, dc in near_peers]
+    barrier = pltpu.get_barrier_semaphore()
+    for _, to_y, to_core in near:
+        pl.semaphore_signal(
+            barrier, 1, device_id=device_at(to_y, z, to_core), device_id_type=MESH
+        )
+    for step in range(1, ring):
+        pl.semaphore_signal(
+            barrier, 1, device_id=device_at(y, (z + step) % ring, core), device_id_type=MESH
+        )
+    rounded[...] = gradient[...].astype(jnp.bfloat16)
+    pl.semaphore_wait(barrier, len(near) + ring - 1)
+
+    near_copies = []
+    for slot, to_y, to_core in near:
+        row = pl.multiple_of((to_y * 2 + to_core) * rows, rows)
+        copy = pltpu.make_async_remote_copy(
+            src_ref=rounded.at[pl.ds(row, rows)],
+            dst_ref=near_in.at[slot],
+            send_sem=near_send.at[slot],
+            recv_sem=near_recv.at[slot],
+            device_id=device_at(to_y, z, to_core),
+            device_id_type=MESH,
+        )
+        copy.start()
+        near_copies.append((slot, copy))
+    own = pl.multiple_of((y * 2 + core) * rows, rows)
+    value = gradient[pl.ds(own, rows), :]
+    for slot, copy in near_copies:
+        copy.wait_recv()
+        value = value + near_in[slot].astype(jnp.float32)
+    for part in range(ring):
+        row, column = (part % 8) * 8, (part // 8) * 128
+        piece[part] = value[row : row + 8, column : column + 128]
+
+    far_copies = []
+    for step in range(1, ring):
+        to_z = (z + step) % ring
+        copy = pltpu.make_async_remote_copy(
+            src_ref=piece.at[to_z],
+            dst_ref=far_in.at[step],
+            send_sem=far_send.at[step],
+            recv_sem=far_recv.at[step],
+            device_id=device_at(y, to_z, core),
+            device_id_type=MESH,
+        )
+        copy.start()
+        far_copies.append(copy)
+    part_total = piece[z]
+    for step, copy in enumerate(far_copies, 1):
+        copy.wait_recv()
+        part_total = part_total + far_in[step]
+    all_parts[z] = part_total
+
+    back_copies = []
+    for step in range(1, ring):
+        copy = pltpu.make_async_remote_copy(
+            src_ref=all_parts.at[z],
+            dst_ref=all_parts.at[z],
+            send_sem=back_send.at[step],
+            recv_sem=back_recv.at[step],
+            device_id=device_at(y, (z + step) % ring, core),
+            device_id_type=MESH,
+        )
+        copy.start()
+        back_copies.append(copy)
+    for copy in back_copies:
+        copy.wait_recv()
+    for part in range(ring):
+        row, column = (part % 8) * 8, (part // 8) * 128
+        joined[pl.ds(pl.multiple_of(own + row, 8), 8), column : column + 128] = all_parts[part]
+    rounded_own = joined[pl.ds(own, rows), :].astype(jnp.bfloat16)
+    total[pl.ds(own, rows), :] = rounded_own
+
+    last_copies = []
+    for slot, to_y, to_core in near:
+        copy = pltpu.make_async_remote_copy(
+            src_ref=total.at[pl.ds(own, rows)],
+            dst_ref=total.at[pl.ds(own, rows)],
+            send_sem=last_send.at[slot],
+            recv_sem=last_recv.at[slot],
+            device_id=device_at(to_y, z, to_core),
+            device_id_type=MESH,
+        )
+        copy.start()
+        last_copies.append(copy)
+    for copy in last_copies:
+        copy.wait_recv()
+    for _, copy in near_copies:
+        copy.wait_send()
+    for copy in far_copies + back_copies + last_copies:
+        copy.wait_send()
+
+
+def summed_over_trainer(gradient, collective_id):
+    height, width = gradient.shape
+    dma = pltpu.SemaphoreType.DMA
+    return pl.pallas_call(
+        sum_kernel,
+        out_shape=jax.ShapeDtypeStruct((height, width), jnp.bfloat16),
+        in_specs=[pl.BlockSpec(memory_space=pltpu.VMEM)],
+        out_specs=pl.BlockSpec(memory_space=pltpu.VMEM),
+        scratch_shapes=[
+            pltpu.VMEM((height, width), jnp.bfloat16),
+            pltpu.VMEM((8, height // 8, width), jnp.bfloat16),
+            pltpu.VMEM((ring, 8, 128), jnp.float32),
+            pltpu.VMEM((ring, 8, 128), jnp.float32),
+            pltpu.VMEM((ring, 8, 128), jnp.float32),
+            pltpu.VMEM((height, width), jnp.float32),
+            dma((8,)),
+            dma((8,)),
+            dma((ring,)),
+            dma((ring,)),
+            dma((ring,)),
+            dma((ring,)),
+            dma((8,)),
+            dma((8,)),
+        ],
+        compiler_params=pltpu.CompilerParams(collective_id=collective_id, has_side_effects=True),
+    )(gradient)
+
+
+def take_step(master, gradient, collective_id):
+    total = summed_over_trainer(gradient, collective_id).astype(jnp.float32)
     return master - step_length * total / jnp.sqrt(jnp.sum(total * total) + epsilon)
 
 
@@ -102,7 +260,7 @@
     )
     first_memory = node_memory.at[target_ids[0, 0]].set(first_fresh)
     second_memory = passed_along(first_memory, "epoch", 1)
-    master = take_step(master, first_gradient)
+    master = take_step(master, first_gradient, 0)
     second_fresh, second_aggregate = fresh_memory(
         second_memory,
         neighbour_ids,
@@ -122,7 +280,7 @@
         second_aggregate,
         master.astype(jnp.bfloat16),
     )
-    master = take_step(master, second_gradient)
+    master = take_step(master, second_gradient, 1)
     logit_rows = jnp.stack([first_positive, first_negative, second_positive, second_negative])
     return (final_memory[None], master[None], logit_rows[None])
 

time: 759 us -> 198 us (0.26)
  waiting for transfers between devices: 641 us -> 0.01 us
  Pallas kernels: 0 us -> 76 us
  other arithmetic: 28.8 us -> 44.5 us
  between operations: 16 us -> 3.12 us
    psum x2 -> x0, waiting for transfers between devices: 641 us -> none  [take_step(): total = lax.psum(gradient, ('batch', 'mem'))]
    pallas_call x0 -> x2, Pallas kernels: none -> 76 us  [summed_over_trainer(): pl.pallas_call(sum_kernel, out_shape=jax.ShapeDtypeStruct((height, width)...]
  transfers between devices with their start and end apart: 3 -> 1, of which waited for: 2 -> 0; matrix products, arithmetic and copies ran while one was open for 3% -> 19% of each run, Pallas kernels for 0% -> 23%
where the time goes in v1:
time: 198 us; the launch traced here: 197 us
  Pallas kernels  76 us (38%)
  local copies, waits for them, and re-layouts  57.7 us (29%)
  other arithmetic  44.5 us (22%)
  matrix products  11.6 us (6%)
  starting transfers between devices  3.95 us (2%)
  between operations  3.12 us (2%)
    pallas_call x2, Pallas kernels, summed_over_trainer(): pl.pallas_call(sum_kernel, out_shape=jax.ShapeDtypeStruct((height, width)...  76 us
    gather x20, local copies, waits for them, and re-layouts, fresh_memory(): near_rows = jnp.take(memory_block, near_ids[slot], axis=0)  36.7 us
    gather x26, other arithmetic  8.83 us
    and x10, other arithmetic, fresh_memory(): near_rows = jnp.take(memory_block, near_ids[slot], axis=0)  8.05 us
    dot_general x2, matrix products, fresh_memory(): jnp.dot(target_rows, gru_state, preferred_element_type=jnp.float32)  4.95 us
    convert_element_type x2, other arithmetic, link_terms(): (0.5 * (target_rows.astype(jnp.float32) + aggregate)).astype(jnp.bfloat16)  4.1 us
    unnamed x112, local copies, waits for them, and re-layouts  3.97 us
  transfers between devices with their start and end apart: 1, of which 0 were waited for; matrix products, arithmetic and copies ran while one was open for 19% of the time, Pallas kernels for 23%

profile of v1, /device:TPU:1, one launch (start us, length us, event | category | flops | bytes accessed | tf_op | source)
XLA Modules:
  0.0 196.9 jit_solution(9766283406863505303)
XLA Ops:
  9.5 1.9 gather_fusion.14
  11.4 1.9 gather_fusion.13
  13.2 1.8 gather_fusion.12
  15.1 1.9 gather_fusion.11
  18.8 1.9 gather_fusion.9
  20.6 1.9 gather_fusion.8
  22.5 1.9 gather_fusion.7
  24.4 1.9 gather_fusion.6
  28.5 1.9 gather_fusion.15
  34.0 3.6 %scatter_custom_fusion = bf16[512,512]{1,0:T(8,128)(2,1)S(1)} fusion(bf16[512,512]{1,0:T(8,128)(2,1)S(1)} %copy.25, s32[256]{0:T(256)S(1)} %bitcast.74, f32[256,1536]{1,0:T(8,128)} %fusion.68, f32[256,1536]{1,0:T(8,128)} %fusion.78, f32[]{:T(128)} %constant.27.clone.1, bf16[256,512]{1,0:T(8,128)(2,1)S(1)} %gather_fusion.1, ...), kind=kCustom, calls=%fused_computation.117 | custom fusion | flops 2228224 | bytes 3932676 | tf_op jit(solution)/shard_map/scatter | solution.py:261
  37.6 4.0 %collective-permute-start = (bf16[512,512]{1,0:T(8,128)(2,1)S(1)}, bf16[512,512]{1,0:T(8,128)(2,1)S(1)}, u32[]{:S(2)}, u32[]{:S(2)}) collective-permute-start(bf16[512,512]{1,0:T(8,128)(2,1)S(1)} %scatter_custom_fusion), channel_id=1, source_target_pairs={{0,128},{128,256},{256,384},{384,0},{1,129},{129,257},{257,385},{3... | collective-permute-start | bytes 1572872 | tf_op jit(solution)/shard_map/ppermute | solution.py:15
  77.2 45.2 %shard_map.121 = bf16[512,256]{1,0:T(8,128)(2,1)} custom-call(f32[512,256]{1,0:T(8,128)} %fusion.37.gradient), custom_call_target="tpu_custom_call" | custom-call | tf_op jit(solution)/shard_map/pallas_call | solution.py:200
  131.0 3.2 %fusion.69 = f32[256,1536]{1,0:T(8,128)} fusion(bf16[512,1536]{1,0:T(8,128)(2,1)} %param.22, bf16[256,512]{1,0:T(8,128)(2,1)S(1)} %gather_fusion.3, pred[256]{0:T(512)(128)(4,1)S(1)} %compare_and_fusion.22), kind=kOutput, calls=%fused_computation.263 | convolution fusion | flops 402784256 | bytes 3408128 | tf_op jit(solution)/shard_map/dot_general | solution.py:31
  136.6 2.0 %gather_fusion.26 = bf16[256,512]{1,0:T(8,128)(2,1)} fusion(bf16[512,512]{1,0:T(8,128)(2,1)S(1)} %collective-permute-done, s32[1024]{0:T(1024)} %pad_clamp_fusion.3), kind=kCustom, calls=%fused_computation.23.clone | custom fusion | bytes 525312 | tf_op jit(solution)/shard_map/jit(_take)/gather | solution.py:27
  138.6 2.0 %gather_fusion.25 = bf16[256,512]{1,0:T(8,128)(2,1)} fusion(bf16[512,512]{1,0:T(8,128)(2,1)S(1)} %collective-permute-done, s32[1024]{0:T(1024)} %pad_clamp_fusion.4), kind=kCustom, calls=%fused_computation.22.clone | custom fusion | bytes 525312 | tf_op jit(solution)/shard_map/jit(_take)/gather | solution.py:27
  140.6 2.0 %gather_fusion.24 = bf16[256,512]{1,0:T(8,128)(2,1)} fusion(bf16[512,512]{1,0:T(8,128)(2,1)S(1)} %collective-permute-done, s32[1024]{0:T(1024)} %pad_clamp_fusion.5), kind=kCustom, calls=%fused_computation.21.clone | custom fusion | bytes 525312 | tf_op jit(solution)/shard_map/jit(_take)/gather | solution.py:27
  142.6 2.0 %gather_fusion.23 = bf16[256,512]{1,0:T(8,128)(2,1)} fusion(bf16[512,512]{1,0:T(8,128)(2,1)S(1)} %collective-permute-done, s32[1024]{0:T(1024)} %pad_clamp_fusion.6), kind=kCustom, calls=%fused_computation.20.clone | custom fusion | bytes 525312 | tf_op jit(solution)/shard_map/jit(_take)/gather | solution.py:27
  146.4 2.0 %gather_fusion.21 = bf16[256,512]{1,0:T(8,128)(2,1)} fusion(bf16[512,512]{1,0:T(8,128)(2,1)S(1)} %collective-permute-done, s32[1024]{0:T(1024)} %pad_clamp_fusion.8), kind=kCustom, calls=%fused_computation.18.clone | custom fusion | bytes 525312 | tf_op jit(solution)/shard_map/jit(_take)/gather | solution.py:27
  148.4 2.0 %gather_fusion.20 = bf16[256,512]{1,0:T(8,128)(2,1)} fusion(bf16[512,512]{1,0:T(8,128)(2,1)S(1)} %collective-permute-done, s32[1024]{0:T(1024)} %pad_clamp_fusion.9), kind=kCustom, calls=%fused_computation.17.clone | custom fusion | bytes 525312 | tf_op jit(solution)/shard_map/jit(_take)/gather | solution.py:27
  150.4 1.9 gather_fusion.19
  152.4 2.7 %fusion.7 = bf16[256,512]{1,0:T(8,128)(2,1)S(1)} fusion(bf16[256,512]{1,0:T(8,128)(2,1)S(1)} %gather_fusion.28, bf16[256,512]{1,0:T(8,128)(2,1)S(1)} %gather_fusion.27, bf16[256,512]{1,0:T(8,128)(2,1)} %gather_fusion.26, bf16[256,512]{1,0:T(8,128)(2,1)} %gather_fusion.25, bf16[256,512]{1,0:T(8,128)(2,1)} %gather_fusion.24, ...), kind=kLoop, calls=%fused_computation.49 | loop fusion | flops 5898240 | bytes 3159808 | tf_op jit(solution)/shard_map/convert_element_type | solution.py:46
  157.0 30.7 %shard_map.122 = bf16[512,256]{1,0:T(8,128)(2,1)} custom-call(f32[512,256]{1,0:T(8,128)} %fusion.43.gradient), custom_call_target="tpu_custom_call" | custom-call | tf_op jit(solution)/shard_map/pallas_call | solution.py:200
  190.1 1.9 fusion.13
  192.0 3.4 %scatter_custom_fusion.1 = bf16[512,512]{1,0:T(8,128)(2,1)S(1)} fusion(bf16[512,512]{1,0:T(8,128)(2,1)S(1)} %collective-permute-done, s32[256]{0:T(256)} %bitcast.73, f32[256,1536]{1,0:T(8,128)} %fusion.69, f32[256,1536]{1,0:T(8,128)} %fusion.79, f32[]{:T(128)} %constant.27.clone.1, bf16[256,512]{1,0:T(8,128)(2,1)S(1)} %gather_fusion.3, ...), kind=kCustom, calls=%fused_computation.116 | custom fusion | flops 2228224 | bytes 3933184 | tf_op jit(solution)/shard_map/scatter | solution.py:274
  (219 shorter events, 68.4 us)
Async XLA Ops:
  0.6 29.9 %copy-start = (bf16[512,1536]{1,0:T(8,128)(2,1)S(1)}, bf16[512,1536]{1,0:T(8,128)(2,1)}, u32[]{:S(2)}) copy-start(bf16[512,1536]{1,0:T(8,128)(2,1)} %param.21) | copy-start | bytes 4718596
  8.0 3.3 %copy-start.23 = (s32[256]{0:T(256)}, s32[256]{0:T(256)S(1)}, u32[]{:S(2)}) copy-start(s32[256]{0:T(256)S(1)} %get-tuple-element.26) | copy-start | bytes 3076
  8.0 3.3 %copy-start.24 = (s32[256]{0:T(256)}, s32[256]{0:T(256)S(1)}, u32[]{:S(2)}) copy-start(s32[256]{0:T(256)S(1)} %get-tuple-element.27) | copy-start | bytes 3076
  8.0 3.3 %copy-start.25 = (s32[256]{0:T(256)}, s32[256]{0:T(256)S(1)}, u32[]{:S(2)}) copy-start(s32[256]{0:T(256)S(1)} %get-tuple-element.24) | copy-start | bytes 3076
  8.0 3.3 %copy-start.26 = (s32[256]{0:T(256)}, s32[256]{0:T(256)S(1)}, u32[]{:S(2)}) copy-start(s32[256]{0:T(256)S(1)} %get-tuple-element.25) | copy-start | bytes 3076
  8.0 3.3 %copy-start.27 = (s32[256]{0:T(256)}, s32[256]{0:T(256)S(1)}, u32[]{:S(2)}) copy-start(s32[256]{0:T(256)S(1)} %get-tuple-element.22) | copy-start | bytes 3076
  8.0 3.3 %copy-start.28 = (s32[256]{0:T(256)}, s32[256]{0:T(256)S(1)}, u32[]{:S(2)}) copy-start(s32[256]{0:T(256)S(1)} %get-tuple-element.23) | copy-start | bytes 3076
  8.1 3.3 %copy-start.29 = (s32[256]{0:T(256)}, s32[256]{0:T(256)S(1)}, u32[]{:S(2)}) copy-start(s32[256]{0:T(256)S(1)} %get-tuple-element.20) | copy-start | bytes 3076
  8.1 3.3 %copy-start.30 = (s32[256]{0:T(256)}, s32[256]{0:T(256)S(1)}, u32[]{:S(2)}) copy-start(s32[256]{0:T(256)S(1)} %get-tuple-element.21) | copy-start | bytes 3076
  8.1 3.3 %copy-start.31 = (s32[256]{0:T(256)}, s32[256]{0:T(256)S(1)}, u32[]{:S(2)}) copy-start(s32[256]{0:T(256)S(1)} %get-tuple-element.19) | copy-start | bytes 3076
  8.1 3.3 %copy-start.32 = (s32[256]{0:T(256)}, s32[256]{0:T(256)S(1)}, u32[]{:S(2)}) copy-start(s32[256]{0:T(256)S(1)} %get-tuple-element.28) | copy-start | bytes 3076
  37.6 87.3 %collective-permute-start = (bf16[512,512]{1,0:T(8,128)(2,1)S(1)}, bf16[512,512]{1,0:T(8,128)(2,1)S(1)}, u32[]{:S(2)}, u32[]{:S(2)}) collective-permute-start(bf16[512,512]{1,0:T(8,128)(2,1)S(1)} %scatter_custom_fusion), channel_id=1, source_target_pairs={{0,128},{128,256},{256,384},{384,0},{1,129},{129,257},{257,385},{3... | collective-permute-start | bytes 1572872 | tf_op jit(solution)/shard_map/ppermute | solution.py:15
  70.1 3.5 %copy-start.53 = (pred[256]{0:T(512)(128)(4,1)S(1)}, pred[256]{0:T(512)(128)(4,1)}, u32[]{:S(2)}) copy-start(pred[256]{0:T(512)(128)(4,1)} %compare_and_fusion.11) | copy-start | bytes 772
  75.9 48.9 %copy-start.34 = (s32[256]{0:T(256)S(1)}, s32[256]{0:T(256)}, u32[]{:S(2)}) copy-start(s32[256]{0:T(256)} %get-tuple-element.86) | copy-start | bytes 3076
  75.9 48.9 %copy-start.21 = (s32[256]{0:T(256)S(1)}, s32[256]{0:T(256)}, u32[]{:S(2)}) copy-start(s32[256]{0:T(256)} %get-tuple-element.44) | copy-start | bytes 3076
  75.9 48.9 %copy-start.22 = (s32[256]{0:T(256)S(1)}, s32[256]{0:T(256)}, u32[]{:S(2)}) copy-start(s32[256]{0:T(256)} %get-tuple-element.45) | copy-start | bytes 3076
  76.0 48.9 %copy-start.19 = (s32[256]{0:T(256)S(1)}, s32[256]{0:T(256)}, u32[]{:S(2)}) copy-start(s32[256]{0:T(256)} %get-tuple-element.46) | copy-start | bytes 3076
  76.0 48.9 %copy-start.20 = (s32[256]{0:T(256)S(1)}, s32[256]{0:T(256)}, u32[]{:S(2)}) copy-start(s32[256]{0:T(256)} %get-tuple-element.47) | copy-start | bytes 3076
  150.4 1.9 copy-start.38
  150.4 1.9 copy-start.39
  152.4 2.8 %copy-start.2 = (bf16[512,256]{1,0:T(8,128)(2,1)S(1)}, bf16[512,256]{1,0:T(8,128)(2,1)}, u32[]{:S(2)}) copy-start(bf16[512,256]{1,0:T(8,128)(2,1)} %shard_map.121) | copy-start | bytes 786436
  152.4 2.8 %copy-start.15 = (bf16[256,512]{1,0:T(8,128)(2,1)S(1)}, bf16[256,512]{1,0:T(8,128)(2,1)}, u32[]{:S(2)}) copy-start(bf16[256,512]{1,0:T(8,128)(2,1)} %get-tuple-element.119) | copy-start | bytes 786436
  152.4 2.8 %copy-start.17 = (bf16[512,256]{1,0:T(8,128)(2,1)S(1)}, bf16[512,256]{1,0:T(8,128)(2,1)}, u32[]{:S(2)}) copy-start(bf16[512,256]{1,0:T(8,128)(2,1)} %param.23) | copy-start | bytes 786436
  155.8 34.3 %copy-start.18 = (bf16[512,256]{1,0:T(8,128)(2,1)S(1)}, bf16[512,256]{1,0:T(8,128)(2,1)}, u32[]{:S(2)}) copy-start(bf16[512,256]{1,0:T(8,128)(2,1)} %param.23) | copy-start | bytes 786436
  (31 other events, 54.9 us)

commit v2 on v0

v2 whole, which is shorter than its diff:
```python
import jax
import jax.numpy as jnp
from jax import lax
from jax.experimental import pallas as pl
from jax.experimental.pallas import tpu as pltpu
from jax.sharding import PartitionSpec as P

MESH = pl.DeviceIdType.MESH
bf16, f32 = jnp.bfloat16, jnp.float32
tick_scale = 100.0
step_length = 4.0
epsilon = 1e-06
near_count, far_count = 16, 8


def matmul(a, b):
    return jnp.dot(a, b, preferred_element_type=f32)


def matmul_nt(a, b):
    return lax.dot_general(a, b, (((1,), (1,)), ((), ())), preferred_element_type=f32)


def device_at(y, z, core):
    return {"batch": y * 8 + z % 8, "mem": (z // 8) * 2 + core}


class Place:
    def __init__(self):
        self.epoch = lax.axis_index("epoch")
        batch, mem = lax.axis_index("batch"), lax.axis_index("mem")
        self.y, self.core = batch // 8, mem % 2
        z = (mem // 2) * 8 + batch % 8
        self.pair, self.side = z // 2, z % 2
        self.piece = (self.y * 2 + self.core) * 2 + self.side

    def near(self, step):
        y, core = (self.y + step // 4) % 4, (self.core + (step // 2) % 2) % 2
        side = (self.side + step % 2) % 2
        return device_at(y, self.pair * 2 + side, core), (y * 2 + core) * 2 + side

    def far(self, step):
        return device_at(self.y, ((self.pair + step) % far_count) * 2 + self.side, self.core)

    def next_epoch(self):
        return {"epoch": (self.epoch + 1) % 4}

    def last_epoch(self):
        return {"epoch": (self.epoch + 3) % 4}


near_steps = sorted(range(1, near_count), key=lambda k: -(min(k // 4, 4 - k // 4) + k % 2))
far_steps = (4, 3, 5, 2, 6, 1, 7)


class TrainerSum:
    def __init__(self, place, gradient, rounded, near_in, far_in, total, sems):
        self.place, self.gradient, self.rounded = place, gradient, rounded
        self.near_in, self.far_in, self.total, self.sems = near_in, far_in, total, sems
        self.own = pl.ds(pl.multiple_of(place.piece * 16, 16), 16)
        self.copies = []

    def send(self, src, dst, stage, step, device):
        copy = pltpu.make_async_remote_copy(
            src_ref=src,
            dst_ref=dst,
            send_sem=self.sems.at[2 * stage, step],
            recv_sem=self.sems.at[2 * stage + 1, step],
            device_id=device,
            device_id_type=MESH,
        )
        copy.start()
        self.copies.append(copy)
        return copy

    def scatter(self):
        self.pending = []
        for step in near_steps:
            device, piece = self.place.near(step)
            rows = pl.ds(pl.multiple_of(piece * 16, 16), 16)
            copy = self.send(self.rounded.at[rows], self.near_in.at[step], 0, step, device)
            self.pending.append((step, copy))

    def exchange(self):
        value = self.gradient[self.own, :]
        for step, copy in reversed(self.pending):
            copy.wait_recv()
            value = value + self.near_in[step].astype(f32)
        slot = self.far_in.at[self.place.pair]
        slot[...] = value.astype(bf16)
        self.pending = [
            self.send(slot, slot, 1, step, self.place.far(step)) for step in far_steps
        ]

    def gather(self):
        for copy in self.pending:
            copy.wait_recv()
        value = self.far_in[0].astype(f32)
        for slot in range(1, far_count):
            value = value + self.far_in[slot].astype(f32)
        self.total[self.own, :] = value.astype(bf16)
        rows = self.total.at[self.own]
        self.pending = [
            self.send(rows, rows, 2, step, self.place.near(step)[0]) for step in near_steps
        ]

    def arrive(self):
        for copy in self.pending:
            copy.wait_recv()

    def close(self):
        for copy in self.copies:
            copy.wait_send()


def column_picks(column, count):
    lanes = lax.broadcasted_iota(jnp.int32, (column.shape[0], count), 1).astype(f32)
    return jnp.where(column == lanes, 1.0, 0.0).astype(bf16)


def row_picks(row, count):
    names = lax.broadcasted_iota(jnp.int32, (count, row.shape[1]), 0).astype(f32)
    return jnp.where(row == names, 1.0, 0.0)


def neighbour_weights(target_picks, ticks, near_ids, near_times):
    def looked_up(table):
        low = (table & 255).astype(f32).astype(bf16)
        high = (table >> 8).astype(f32).astype(bf16)
        return matmul_nt(target_picks, low) + 256.0 * matmul_nt(target_picks, high)

    ids, times = looked_up(near_ids), looked_up(near_times)
    decay = tick_scale / (tick_scale + (ticks - times))
    decay = decay / jnp.sum(decay, axis=1, keepdims=True)
    events, nodes = target_picks.shape
    lanes = lax.broadcasted_iota(jnp.int32, (events, nodes), 1).astype(f32)
    weights = jnp.zeros((events, nodes), f32)
    for slot in range(near_ids.shape[0]):
        chosen = ids[:, slot : slot + 1] == lanes
        weights = weights + jnp.where(chosen, decay[:, slot : slot + 1], 0.0)
    return weights


def gather_events(memory, columns, near_ids, near_times, stacked, target_rows):
    source, target, negative, ticks = columns
    events, nodes = source.shape[0], memory.shape[0]
    target_picks = column_picks(target, nodes)
    stacked[0:events, :] = matmul(column_picks(source, nodes), memory[...]).astype(bf16)
    stacked[2 * events :, :] = matmul(column_picks(negative, nodes), memory[...]).astype(bf16)
    rows = matmul(target_picks, memory[...])
    target_rows[...] = rows.astype(bf16)
    weights = neighbour_weights(target_picks, ticks, near_ids, near_times)
    high = weights.astype(bf16)
    low = (weights - high.astype(f32)).astype(bf16)
    aggregate = matmul(high, memory[...]) + matmul(low, memory[...])
    stacked[events : 2 * events, :] = (0.5 * (rows + aggregate)).astype(bf16)


def link_gradient(stacked, projection, logits, row, deltas, gradient, rounded):
    events = stacked.shape[0] // 3
    scale = 1.0 / projection.shape[0] ** 0.5
    projected = matmul_nt(projection, stacked[...])
    source = projected[:, :events]
    target = projected[:, events : 2 * events]
    negative = projected[:, 2 * events :]
    positive = jnp.sum(source * target, axis=0, keepdims=True) * scale
    negative_logit = jnp.sum(source * negative, axis=0, keepdims=True) * scale
    logits[0, row : row + 1, :] = positive
    logits[0, row + 1 : row + 2, :] = negative_logit
    grad_positive = -jax.nn.sigmoid(-positive) * scale
    grad_negative = jax.nn.sigmoid(negative_logit) * scale
    deltas[:, :events] = (grad_positive * target + grad_negative * negative).astype(bf16)
    deltas[:, events : 2 * events] = (grad_positive * source).astype(bf16)
    deltas[:, 2 * events :] = (grad_negative * source).astype(bf16)
    value = matmul(deltas[...], stacked[...])
    gradient[...] = value
    rounded[...] = value.astype(bf16)


def fresh_rows(source_rows, target_rows, gru_input, gru_state):
    width = source_rows.shape[1]

    def gate(weights, rows, part):
        return matmul(rows, weights[:, part * width : (part + 1) * width])

    reset = jax.nn.sigmoid(gate(gru_input, source_rows, 0) + gate(gru_state, target_rows, 0))
    candidate = jnp.tanh(
        gate(gru_input, source_rows, 2) + reset * gate(gru_state, target_rows, 2)
    )
    update = jax.nn.sigmoid(gate(gru_input, source_rows, 1) + gate(gru_state, target_rows, 1))
    return ((1.0 - update) * candidate + update * target_rows.astype(f32)).astype(bf16)


def replaced(memory, target_row, fresh):
    picks = row_picks(target_row, memory.shape[0])
    hit = jnp.sum(picks, axis=1, keepdims=True)
    placed = matmul(picks.astype(bf16), fresh)
    return jnp.where(hit > 0.5, placed, memory[...].astype(f32)).astype(bf16)


def stepped(master, total):
    total = total[...].astype(f32)
    return master - step_length * total / jnp.sqrt(jnp.sum(total * total) + epsilon)


def window_kernel(
    memory_hbm,
    near_ids_hbm,
    near_times_hbm,
    source_ids_hbm,
    target_ids_hbm,
    negative_ids_hbm,
    event_ticks_hbm,
    gru_input_hbm,
    gru_state_hbm,
    decoder_hbm,
    memory_out,
    decoder_out,
    logits_out,
    memory,
    near_ids,
    near_times,
    source_ids,
    target_ids,
    negative_ids,
    event_ticks,
    gru_input,
    gru_state,
    decoder,
    handed_source,
    handed_target,
    handed_memory,
    stacked,
    target_rows,
    deltas,
    master,
    gradient,
    rounded,
    near_in,
    far_in,
    total,
    load_sems,
    hand_sems,
    sum_sems,
):
    loads = [
        pltpu.make_async_copy(stored, held, load_sems.at[slot])
        for slot, (stored, held) in enumerate(
            (
                (source_ids_hbm, source_ids),
                (target_ids_hbm, target_ids),
                (negative_ids_hbm, negative_ids),
                (event_ticks_hbm, event_ticks),
                (near_ids_hbm, near_ids),
                (near_times_hbm, near_times),
                (decoder_hbm, decoder),
                (memory_hbm, memory),
                (gru_input_hbm, gru_input),
                (gru_state_hbm, gru_state),
            )
        )
    ]
    for load in loads:
        load.start()
    place = Place()
    barrier = pltpu.get_barrier_semaphore()
    greeted = [place.near(step)[0] for step in near_steps]
    greeted += [place.far(step) for step in far_steps]
    greeted += [place.next_epoch(), place.last_epoch()]
    for device in greeted:
        pl.semaphore_signal(barrier, 1, device_id=device, device_id_type=MESH)

    for load in loads[:8]:
        load.wait()
    ids = jnp.concatenate(
        [source_ids[0], target_ids[0], negative_ids[0], event_ticks[0]], axis=0
    ).astype(f32)
    columns = ids.T
    first_columns = [columns[:, 2 * kind : 2 * kind + 1] for kind in range(4)]
    second_columns = [columns[:, 2 * kind + 1 : 2 * kind + 2] for kind in range(4)]
    master[...] = decoder[...].astype(f32).T
    near_id_table, near_time_table = near_ids[...], near_times[...]

    gather_events(memory, first_columns, near_id_table, near_time_table, stacked, target_rows)
    link_gradient(
        stacked, master[...].astype(bf16), logits_out, 0, deltas, gradient, rounded.at[0]
    )
    pl.semaphore_wait(barrier, len(greeted))

    hands = []
    for slot, (kept, handed) in enumerate(
        ((source_ids, handed_source), (target_ids, handed_target))
    ):
        copy = pltpu.make_async_remote_copy(
            src_ref=kept.at[0],
            dst_ref=handed,
            send_sem=hand_sems.at[0, slot],
            recv_sem=hand_sems.at[1, slot],
            device_id=place.next_epoch(),
            device_id_type=MESH,
        )
        copy.start()
        hands.append(copy)
    sums = [
        TrainerSum(
            place,
            gradient,
            rounded.at[batch],
            near_in.at[batch],
            far_in.at[batch],
            total.at[batch],
            sum_sems.at[batch],
        )
        for batch in range(2)
    ]
    sums[0].scatter()
    for hand in hands:
        hand.wait_recv()
    for load in loads[8:]:
        load.wait()
    handed_rows = jnp.concatenate(
        [handed_source[...], handed_target[...], handed_source[...], handed_target[...]], axis=0
    ).astype(f32)
    handed_columns = handed_rows.T
    nodes = memory.shape[0]
    source = matmul(column_picks(handed_columns[:, 0:1], nodes), memory[...]).astype(bf16)
    target = matmul(column_picks(handed_columns[:, 2:3], nodes), memory[...]).astype(bf16)
    fresh = fresh_rows(source, target, gru_input, gru_state)
    sums[0].exchange()

    handed_memory[...] = replaced(memory, handed_rows[2:3, :], fresh)
    gather_events(
        handed_memory, second_columns, near_id_table, near_time_table, stacked, target_rows
    )
    sums[0].gather()
    sums[0].arrive()

    master[...] = stepped(master[...], total.at[0])
    link_gradient(
        stacked, master[...].astype(bf16), logits_out, 2, deltas, gradient, rounded.at[1]
    )
    sums[1].scatter()
    events = target_rows.shape[0]
    fresh = fresh_rows(stacked[0:events, :], target_rows[...], gru_input, gru_state)
    sums[1].exchange()
    memory_out[0] = replaced(handed_memory, ids[3:4, :], fresh)
    sums[1].gather()
    sums[1].arrive()
    decoder_out[0] = stepped(master[...], total.at[1]).T
    for hand in hands:
        hand.wait_send()
    for each in sums:
        each.close()


def on_device(
    node_memory,
    neighbour_ids,
    neighbour_ticks,
    source_ids,
    target_ids,
    negative_ids,
    event_ticks,
    gru_input,
    gru_state,
    decoder_weight,
):
    nodes, width = node_memory.shape
    hidden = decoder_weight.shape[1]
    batches, events = source_ids.shape[1:]
    vmem, dma = pltpu.VMEM, pltpu.SemaphoreType.DMA
    held = pl.BlockSpec(memory_space=vmem)
    return pl.pallas_call(
        window_kernel,
        out_shape=(
            jax.ShapeDtypeStruct((1, nodes, width), bf16),
            jax.ShapeDtypeStruct((1, width, hidden), f32),
            jax.ShapeDtypeStruct((1, 2 * batches, events), f32),
        ),
        in_specs=[pl.BlockSpec(memory_space=pltpu.HBM)] * 10,
        out_specs=(held, held, held),
        scratch_shapes=[
            vmem(node_memory.shape, bf16),
            vmem(neighbour_ids.shape, jnp.int32),
            vmem(neighbour_ticks.shape, jnp.int32),
            vmem(source_ids.shape, jnp.int32),
            vmem(target_ids.shape, jnp.int32),
            vmem(negative_ids.shape, jnp.int32),
            vmem(event_ticks.shape, jnp.int32),
            vmem(gru_input.shape, bf16),
            vmem(gru_state.shape, bf16),
            vmem(decoder_weight.shape, bf16),
            vmem((batches, events), jnp.int32),
            vmem((batches, events), jnp.int32),
            vmem((nodes, width), bf16),
            vmem((3 * events, width), bf16),
            vmem((events, width), bf16),
            vmem((hidden, 3 * events), bf16),
            vmem((hidden, width), f32),
            vmem((hidden, width), f32),
            vmem((batches, hidden, width), bf16),
            vmem((batches, near_count, hidden // near_count, width), bf16),
            vmem((batches, far_count, hidden // near_count, width), bf16),
            vmem((batches, hidden, width), bf16),
            dma((10,)),
            dma((2, 2)),
            dma((batches, 6, near_count)),
        ],
        compiler_params=pltpu.CompilerParams(
            collective_id=0, has_side_effects=True, vmem_limit_bytes=60 * 2**20
        ),
        name="window",
    )(
        node_memory,
        neighbour_ids,
        neighbour_ticks,
        source_ids,
        target_ids,
        negative_ids,
        event_ticks,
        gru_input,
        gru_state,
        decoder_weight,
    )


def solution(mesh):
    in_specs = (
        P(("batch", "mem"), None),
        P(None, ("batch", "mem")),
        P(None, ("batch", "mem")),
        P("epoch", None, ("batch", "mem")),
        P("epoch", None, ("batch", "mem")),
        P("epoch", None, ("batch", "mem")),
        P("epoch", None, ("batch", "mem")),
        P(),
        P(),
        P(),
    )
    out_specs = (
        P("epoch", ("batch", "mem"), None),
        P("epoch", None, None),
        P("epoch", None, ("batch", "mem")),
    )
    return jax.shard_map(
        on_device, mesh=mesh, in_specs=in_specs, out_specs=out_specs, check_vma=False
    )
```

time: 759 us -> 66 us (0.09)
  waiting for transfers between devices: 641 us -> 0 us
  Pallas kernels: 0 us -> 60.9 us
  local copies, waits for them, and re-layouts: 56 us -> 4.33 us
  other arithmetic: 28.8 us -> 0 us
  between operations: 16 us -> 0.65 us
  matrix products: 13.1 us -> 0 us
    psum x2 -> x0, waiting for transfers between devices: 641 us -> none  [take_step(): total = lax.psum(gradient, ('batch', 'mem'))]
    pallas_call x0 -> x1, Pallas kernels: none -> 60.9 us  [on_device(): pl.pallas_call(window_kernel, out_shape=(jax.ShapeDtypeStruct((1, nodes,...]
    gather x30 -> x0, local copies, waits for them, and re-layouts: 45.8 us -> none  [the longest x20 35.9 us: fresh_memory(): near_rows = jnp.take(memory_block, near_ids[slot], axis=0)]
    dot_general x8 -> x0, matrix products: 13.1 us -> none  [the longest x2 6.35 us: fresh_memory(): jnp.dot(source_rows, gru_input, preferred_element_type=jnp.float32)]
  transfers between devices with their start and end apart: 3 -> 0, of which waited for: 2 -> 0; matrix products, arithmetic and copies ran while one was open for 3% -> 0% of each run, Pallas kernels for 0% -> 0%
where the time goes in v2:
time: 66 us; the launch traced here: 65.8 us
  Pallas kernels  60.9 us (92%)
  local copies, waits for them, and re-layouts  4.33 us (7%)
    pallas_call x1, Pallas kernels, on_device(): pl.pallas_call(window_kernel, out_shape=(jax.ShapeDtypeStruct((1, nodes,...  60.9 us
    unnamed x5, local copies, waits for them, and re-layouts  4.33 us

profile of v2, /device:TPU:1, one launch (start us, length us, event | category | flops | bytes accessed | tf_op | source)
XLA Modules:
  0.0 65.8 jit_solution(8512040160638403099)
XLA Ops:
  0.6 60.9 %window.1 = (bf16[1,512,512]{2,1,0:T(8,128)(2,1)}, f32[1,512,256]{2,1,0:T(8,128)}, f32[1,4,256]{2,1,0:T(4,128)}) custom-call(bf16[512,512]{1,0:T(8,128)(2,1)} %memory_hbm.1, s32[10,512]{1,0:T(8,128)} %near_ids_hbm.1, s32[10,512]{1,0:T(8,128)} %near_times_hbm.1, s32[1,2,256]{2,1,0:T(2,128)} %source_ids_hbm.1, s32[1,2,256]{2,1,0:T(2,128)} %target_ids_hbm.1, ...), custom_call_target="tpu_custom_call" | custom-call | tf_op jit(solution)/shard_map/window/pallas_call | solution.py:373
  61.5 0.0 copy-start
  61.5 1.9 %copy.16 = bf16[1,512,512]{2,1,0:T(8,128)(2,1)} copy(bf16[1,512,512]{2,1,0:T(8,128)(2,1)} %get-tuple-element.6) | data formatting | bytes 1048576
  63.4 1.9 %copy.17 = f32[1,512,256]{2,1,0:T(8,128)} copy(f32[1,512,256]{2,1,0:T(8,128)} %get-tuple-element.7) | data formatting | bytes 1048576
  65.2 0.0 copy-done
  65.3 0.6 copy.18
Async XLA Ops:
  61.5 3.7 %copy-start = (f32[1,4,256]{2,1,0:T(4,128)S(1)}, f32[1,4,256]{2,1,0:T(4,128)}, u32[]{:S(2)}) copy-start(f32[1,4,256]{2,1,0:T(4,128)} %get-tuple-element.8) | copy-start | bytes 12292

commit v3 on v2

--- a/solution.py
+++ b/solution.py
@@ -165,8 +165,8 @@
     negative = projected[:, 2 * events :]
     positive = jnp.sum(source * target, axis=0, keepdims=True) * scale
     negative_logit = jnp.sum(source * negative, axis=0, keepdims=True) * scale
-    logits[0, row : row + 1, :] = positive
-    logits[0, row + 1 : row + 2, :] = negative_logit
+    logits[row : row + 1, :] = positive
+    logits[row + 1 : row + 2, :] = negative_logit
     grad_positive = -jax.nn.sigmoid(-positive) * scale
     grad_negative = jax.nn.sigmoid(negative_logit) * scale
     deltas[:, :events] = (grad_positive * target + grad_negative * negative).astype(bf16)
@@ -215,7 +215,8 @@
     gru_state_hbm,
     decoder_hbm,
     memory_out,
-    decoder_out,
+    master,
+    last_total,
     logits_out,
     memory,
     near_ids,
@@ -233,7 +234,6 @@
     stacked,
     target_rows,
     deltas,
-    master,
     gradient,
     rounded,
     near_in,
@@ -308,7 +308,7 @@
             rounded.at[batch],
             near_in.at[batch],
             far_in.at[batch],
-            total.at[batch],
+            (total, last_total)[batch],
             sum_sems.at[batch],
         )
         for batch in range(2)
@@ -335,7 +335,7 @@
     sums[0].gather()
     sums[0].arrive()
 
-    master[...] = stepped(master[...], total.at[0])
+    master[...] = stepped(master[...], total)
     link_gradient(
         stacked, master[...].astype(bf16), logits_out, 2, deltas, gradient, rounded.at[1]
     )
@@ -343,42 +343,47 @@
     events = target_rows.shape[0]
     fresh = fresh_rows(stacked[0:events, :], target_rows[...], gru_input, gru_state)
     sums[1].exchange()
-    memory_out[0] = replaced(handed_memory, ids[3:4, :], fresh)
+    memory_out[...] = replaced(handed_memory, ids[3:4, :], fresh)
     sums[1].gather()
     sums[1].arrive()
-    decoder_out[0] = stepped(master[...], total.at[1]).T
     for hand in hands:
         hand.wait_send()
     for each in sums:
         each.close()
 
 
-def on_device(
-    node_memory,
-    neighbour_ids,
-    neighbour_ticks,
-    source_ids,
-    target_ids,
-    negative_ids,
-    event_ticks,
-    gru_input,
-    gru_state,
-    decoder_weight,
-):
+def results_kernel(memory, master, total, logits, memory_out, decoder_out, logits_out, decoder, sems):
+    stores = [
+        pltpu.make_async_copy(memory, memory_out.at[0], sems.at[0]),
+        pltpu.make_async_copy(logits, logits_out.at[0], sems.at[1]),
+        pltpu.make_async_copy(decoder, decoder_out.at[0], sems.at[2]),
+    ]
+    stores[0].start()
+    stores[1].start()
+    decoder[...] = stepped(master[...], total).T
+    stores[2].start()
+    for store in stores:
+        store.wait()
+
+
+def on_device(*given):
+    node_memory, neighbour_ids, neighbour_ticks, source_ids, target_ids, negative_ids = given[:6]
+    event_ticks, gru_input, gru_state, decoder_weight = given[6:]
     nodes, width = node_memory.shape
     hidden = decoder_weight.shape[1]
     batches, events = source_ids.shape[1:]
     vmem, dma = pltpu.VMEM, pltpu.SemaphoreType.DMA
     held = pl.BlockSpec(memory_space=vmem)
-    return pl.pallas_call(
+    kept = pl.pallas_call(
         window_kernel,
         out_shape=(
-            jax.ShapeDtypeStruct((1, nodes, width), bf16),
-            jax.ShapeDtypeStruct((1, width, hidden), f32),
-            jax.ShapeDtypeStruct((1, 2 * batches, events), f32),
+            vmem((nodes, width), bf16),
+            vmem((hidden, width), f32),
+            vmem((hidden, width), bf16),
+            vmem((2 * batches, events), f32),
         ),
         in_specs=[pl.BlockSpec(memory_space=pltpu.HBM)] * 10,
-        out_specs=(held, held, held),
+        out_specs=(held,) * 4,
         scratch_shapes=[
             vmem(node_memory.shape, bf16),
             vmem(neighbour_ids.shape, jnp.int32),
@@ -397,31 +402,32 @@
             vmem((events, width), bf16),
             vmem((hidden, 3 * events), bf16),
             vmem((hidden, width), f32),
-            vmem((hidden, width), f32),
             vmem((batches, hidden, width), bf16),
             vmem((batches, near_count, hidden // near_count, width), bf16),
             vmem((batches, far_count, hidden // near_count, width), bf16),
-            vmem((batches, hidden, width), bf16),
+            vmem((hidden, width), bf16),
             dma((10,)),
             dma((2, 2)),
             dma((batches, 6, near_count)),
         ],
         compiler_params=pltpu.CompilerParams(
-            collective_id=0, has_side_effects=True, vmem_limit_bytes=60 * 2**20
+            collective_id=0, has_side_effects=True, vmem_limit_bytes=50 * 2**20
         ),
         name="window",
-    )(
-        node_memory,
-        neighbour_ids,
-        neighbour_ticks,
-        source_ids,
-        target_ids,
-        negative_ids,
-        event_ticks,
-        gru_input,
-        gru_state,
-        decoder_weight,
-    )
+    )(*(pltpu.with_memory_space_constraint(each, pltpu.HBM) for each in given))
+    stored = pl.BlockSpec(memory_space=pltpu.HBM)
+    return pl.pallas_call(
+        results_kernel,
+        out_shape=(
+            jax.ShapeDtypeStruct((1, nodes, width), bf16),
+            jax.ShapeDtypeStruct((1, width, hidden), f32),
+            jax.ShapeDtypeStruct((1, 2 * batches, events), f32),
+        ),
+        in_specs=[held] * 4,
+        out_specs=(stored,) * 3,
+        scratch_shapes=[vmem((width, hidden), f32), dma((3,))],
+        name="results",
+    )(*kept)
 
 
 def solution(mesh):

time: 66 us -> 65.7 us (level)
  local copies, waits for them, and re-layouts: 4.33 us -> 2.88 us
  Pallas kernels: 60.9 us -> 62 us
    unnamed x5 -> x8, local copies, waits for them, and re-layouts: 4.33 us -> 2.88 us
    pallas_call x1 -> x2, Pallas kernels: 60.9 us -> 62 us  [the longest x1 59.4 us: on_device(): pl.pallas_call(window_kernel, out_shape=(vmem((nodes, width), bf16), vmem...]
where the time goes in v3:
time: 65.7 us; the launch traced here: 65.5 us
  Pallas kernels  62 us (94%)
  local copies, waits for them, and re-layouts  2.88 us (4%)
    pallas_call x1, Pallas kernels, on_device(): pl.pallas_call(window_kernel, out_shape=(vmem((nodes, width), bf16), vmem...  59.4 us
    unnamed x8, local copies, waits for them, and re-layouts  2.88 us
    pallas_call x1, Pallas kernels, on_device(): pl.pallas_call(results_kernel, out_shape=(jax.ShapeDtypeStruct((1, nodes,...  2.59 us

profile of v3, /device:TPU:1, one launch (start us, length us, event | category | flops | bytes accessed | tf_op | source)
XLA Modules:
  0.0 65.5 jit_solution(17916993517570670140)
XLA Ops:
  0.6 59.4 %window.1 = (bf16[512,512]{1,0:T(8,128)(2,1)S(1)}, f32[256,512]{1,0:T(8,128)S(1)}, bf16[256,512]{1,0:T(8,128)(2,1)S(1)}, f32[4,256]{1,0:T(4,128)S(1)}) custom-call(bf16[512,512]{1,0:T(8,128)(2,1)} %memory_hbm.1, s32[10,512]{1,0:T(8,128)} %near_ids_hbm.1, s32[10,512]{1,0:T(8,128)} %near_times_hbm.1, s32[1,2,256]{2,1,0:T(2,128)} %source_ids_hbm.1, ...), custom_call_target="tpu_custom_call" | custom-call | tf_op jit(solution)/shard_map/window/pallas_call | solution.py:377
  60.1 0.0 copy-start
  60.1 0.8 %copy-done = bf16[512,512]{1,0:T(8,128)(2,1)} copy-done((bf16[512,512]{1,0:T(8,128)(2,1)}, bf16[512,512]{1,0:T(8,128)(2,1)S(1)}, u32[]{:S(2)}) %copy-start) | copy-done | bytes 524312
  60.9 0.0 copy-start.1
  60.9 0.8 %copy-done.1 = f32[256,512]{1,0:T(8,128)} copy-done((f32[256,512]{1,0:T(8,128)}, f32[256,512]{1,0:T(8,128)S(1)}, u32[]{:S(2)}) %copy-start.1) | copy-done | bytes 524312
  61.7 0.0 copy-start.2
  61.7 0.7 %copy-done.2 = bf16[256,512]{1,0:T(8,128)(2,1)} copy-done((bf16[256,512]{1,0:T(8,128)(2,1)}, bf16[256,512]{1,0:T(8,128)(2,1)S(1)}, u32[]{:S(2)}) %copy-start.2) | copy-done | bytes 262168
  62.4 0.0 copy-start.3
  62.4 0.6 copy-done.3
  63.0 2.6 %results.1 = (bf16[1,512,512]{2,1,0:T(8,128)(2,1)}, f32[1,512,256]{2,1,0:T(8,128)}, f32[1,4,256]{2,1,0:T(4,128)}) custom-call(bf16[512,512]{1,0:T(8,128)(2,1)} %copy-done, f32[256,512]{1,0:T(8,128)} %copy-done.1, bf16[256,512]{1,0:T(8,128)(2,1)} %copy-done.2, f32[4,256]{1,0:T(4,128)} %copy-done.3), custom_call_target="tpu_custom_call" | custom-call | tf_op jit(solution)/shard_map/results/pallas_call | solution.py:419
Async XLA Ops:
  60.1 0.8 %copy-start = (bf16[512,512]{1,0:T(8,128)(2,1)}, bf16[512,512]{1,0:T(8,128)(2,1)S(1)}, u32[]{:S(2)}) copy-start(bf16[512,512]{1,0:T(8,128)(2,1)S(1)} %get-tuple-element.7.memory) | copy-start | bytes 1572868
  60.9 0.8 %copy-start.1 = (f32[256,512]{1,0:T(8,128)}, f32[256,512]{1,0:T(8,128)S(1)}, u32[]{:S(2)}) copy-start(f32[256,512]{1,0:T(8,128)S(1)} %get-tuple-element.8.master) | copy-start | bytes 1572868
  61.7 0.7 %copy-start.2 = (bf16[256,512]{1,0:T(8,128)(2,1)}, bf16[256,512]{1,0:T(8,128)(2,1)S(1)}, u32[]{:S(2)}) copy-start(bf16[256,512]{1,0:T(8,128)(2,1)S(1)} %get-tuple-element.9.total) | copy-start | bytes 786436
  62.4 0.6 copy-start.3

commit v4 on v3

--- a/solution.py
+++ b/solution.py
@@ -243,10 +243,16 @@
     hand_sems,
     sum_sems,
 ):
+    place = Place()
+    barrier = pltpu.get_barrier_semaphore()
+    greeted = [place.far(step) for step in far_steps]
+    greeted += [place.near(step)[0] for step in near_steps]
+    greeted += [place.next_epoch(), place.last_epoch()]
     loads = [
         pltpu.make_async_copy(stored, held, load_sems.at[slot])
         for slot, (stored, held) in enumerate(
             (
+                (memory_hbm, memory),
                 (source_ids_hbm, source_ids),
                 (target_ids_hbm, target_ids),
                 (negative_ids_hbm, negative_ids),
@@ -254,24 +260,20 @@
                 (near_ids_hbm, near_ids),
                 (near_times_hbm, near_times),
                 (decoder_hbm, decoder),
-                (memory_hbm, memory),
                 (gru_input_hbm, gru_input),
                 (gru_state_hbm, gru_state),
             )
         )
     ]
-    for load in loads:
+    for load in loads[:8]:
         load.start()
-    place = Place()
-    barrier = pltpu.get_barrier_semaphore()
-    greeted = [place.near(step)[0] for step in near_steps]
-    greeted += [place.far(step) for step in far_steps]
-    greeted += [place.next_epoch(), place.last_epoch()]
     for device in greeted:
         pl.semaphore_signal(barrier, 1, device_id=device, device_id_type=MESH)
-
     for load in loads[:8]:
         load.wait()
+    for load in loads[8:]:
+        load.start()
+
     ids = jnp.concatenate(
         [source_ids[0], target_ids[0], negative_ids[0], event_ticks[0]], axis=0
     ).astype(f32)
@@ -426,8 +428,9 @@
         in_specs=[held] * 4,
         out_specs=(stored,) * 3,
         scratch_shapes=[vmem((width, hidden), f32), dma((3,))],
+        compiler_params=pltpu.CompilerParams(vmem_limit_bytes=8 * 2**20),
         name="results",
-    )(*kept)
+    )(*(pltpu.with_memory_space_constraint(each, pltpu.VMEM) for each in kept))
 
 
 def solution(mesh):

time: 65.7 us -> 60.8 us (0.925)
  local copies, waits for them, and re-layouts: 2.88 us -> 0 us
  Pallas kernels: 62 us -> 60 us
    unnamed x8 -> x0, local copies, waits for them, and re-layouts: 2.88 us -> none
    pallas_call x1, Pallas kernels: 2.59 us -> 1.32 us  [on_device(): pl.pallas_call(results_kernel, out_shape=(jax.ShapeDtypeStruct((1, nodes,...]
    pallas_call x1, Pallas kernels: 59.4 us -> 58.7 us  [on_device(): pl.pallas_call(window_kernel, out_shape=(vmem((nodes, width), bf16), vmem...]
where the time goes in v4:
time: 60.8 us; the launch traced here: 60.7 us
  Pallas kernels  60 us (99%)
  between operations  0.64 us (1%)
    pallas_call x1, Pallas kernels, on_device(): pl.pallas_call(window_kernel, out_shape=(vmem((nodes, width), bf16), vmem...  58.7 us
    pallas_call x1, Pallas kernels, on_device(): pl.pallas_call(results_kernel, out_shape=(jax.ShapeDtypeStruct((1, nodes,...  1.32 us

profile of v4, /device:TPU:1, one launch (start us, length us, event | category | flops | bytes accessed | tf_op | source)
XLA Modules:
  0.0 60.7 jit_solution(2776218880078740720)
XLA Ops:
  0.6 58.7 %window.1 = (bf16[512,512]{1,0:T(8,128)(2,1)S(1)}, f32[256,512]{1,0:T(8,128)S(1)}, bf16[256,512]{1,0:T(8,128)(2,1)S(1)}, f32[4,256]{1,0:T(4,128)S(1)}) custom-call(bf16[512,512]{1,0:T(8,128)(2,1)} %memory_hbm.1, s32[10,512]{1,0:T(8,128)} %near_ids_hbm.1, s32[10,512]{1,0:T(8,128)} %near_times_hbm.1, s32[1,2,256]{2,1,0:T(2,128)} %source_ids_hbm.1, ...), custom_call_target="tpu_custom_call" | custom-call | tf_op jit(solution)/shard_map/window/pallas_call | solution.py:379
  59.3 1.3 %results.1 = (bf16[1,512,512]{2,1,0:T(8,128)(2,1)}, f32[1,512,256]{2,1,0:T(8,128)}, f32[1,4,256]{2,1,0:T(4,128)}) custom-call(bf16[512,512]{1,0:T(8,128)(2,1)S(1)} %get-tuple-element.7.memory, f32[256,512]{1,0:T(8,128)S(1)} %get-tuple-element.8.master, bf16[256,512]{1,0:T(8,128)(2,1)S(1)} %get-tuple-element.9.total, f32[4,256]{1,0:T(4,128)S(1)} %get-tuple-element.10.logits), custom_call_target="tpu_custom_call" | custom-call | tf_op jit(solution)/shard_map/results/pallas_call | solution.py:421

commit v5 on v4

--- a/solution.py
+++ b/solution.py
@@ -11,6 +11,7 @@
 step_length = 4.0
 epsilon = 1e-06
 near_count, far_count = 16, 8
+half = far_count // 2
 
 
 def matmul(a, b):
@@ -39,8 +40,14 @@
         side = (self.side + step % 2) % 2
         return device_at(y, self.pair * 2 + side, core), (y * 2 + core) * 2 + side
 
+    def far_pair(self, step):
+        return (self.pair + step + far_count) % far_count
+
     def far(self, step):
-        return device_at(self.y, ((self.pair + step) % far_count) * 2 + self.side, self.core)
+        return device_at(self.y, self.far_pair(step) * 2 + self.side, self.core)
+
+    def mirror(self):
+        return device_at(self.y, (far_count - 1 - self.pair) * 2 + self.side, self.core)
 
     def next_epoch(self):
         return {"epoch": (self.epoch + 1) % 4}
@@ -54,14 +61,15 @@
 
 
 class TrainerSum:
-    def __init__(self, place, gradient, rounded, near_in, far_in, total, sems):
+    def __init__(self, place, gradient, rounded, near_in, far_in, half_sum, total, sems):
         self.place, self.gradient, self.rounded = place, gradient, rounded
-        self.near_in, self.far_in, self.total, self.sems = near_in, far_in, total, sems
+        self.near_in, self.far_in, self.half_sum = near_in, far_in, half_sum
+        self.total, self.sems = total, sems
         self.own = pl.ds(pl.multiple_of(place.piece * 16, 16), 16)
         self.copies = []
 
-    def send(self, src, dst, stage, step, device):
-        copy = pltpu.make_async_remote_copy(
+    def copy_of(self, src, dst, stage, step, device):
+        return pltpu.make_async_remote_copy(
             src_ref=src,
             dst_ref=dst,
             send_sem=self.sems.at[2 * stage, step],
@@ -69,6 +77,9 @@
             device_id=device,
             device_id_type=MESH,
         )
+
+    def send(self, src, dst, stage, step, device):
+        copy = self.copy_of(src, dst, stage, step, device)
         copy.start()
         self.copies.append(copy)
         return copy
@@ -86,17 +97,54 @@
         for step, copy in reversed(self.pending):
             copy.wait_recv()
             value = value + self.near_in[step].astype(f32)
+        place = self.place
+        self.far_in[place.pair] = value.astype(bf16)
+        for step in far_steps:
+
+            @pl.when((place.pair >= half) | (place.far_pair(step) < half))
+            def _(step=step):
+                self.far_copy(step).start()
+
+    def far_copy(self, step):
         slot = self.far_in.at[self.place.pair]
-        slot[...] = value.astype(bf16)
-        self.pending = [
-            self.send(slot, slot, 1, step, self.place.far(step)) for step in far_steps
-        ]
+        return self.copy_of(slot, slot, 1, step, self.place.far(step))
+
+    def bridge_copy(self):
+        return self.copy_of(self.half_sum, self.half_sum, 1, 0, self.place.mirror())
+
+    def bridge(self, greeting):
+        place = self.place
+
+        @pl.when(place.pair < half)
+        def _():
+            for step in far_steps:
+
+                @pl.when(place.far_pair(-step) < half)
+                def _(step=step):
+                    self.far_copy(step).wait_recv()
+
+            value = self.far_in[0].astype(f32)
+            for slot in range(1, half):
+                value = value + self.far_in[slot].astype(f32)
+            self.half_sum[...] = value.astype(bf16)
+            if greeting is not None:
+                pl.semaphore_wait(greeting, 1)
+            self.bridge_copy().start()
 
     def gather(self):
-        for copy in self.pending:
-            copy.wait_recv()
-        value = self.far_in[0].astype(f32)
-        for slot in range(1, far_count):
+        place = self.place
+        for step in far_steps:
+
+            @pl.when(place.far_pair(-step) >= half)
+            def _(step=step):
+                self.far_copy(step).wait_recv()
+
+        @pl.when(place.pair >= half)
+        def _():
+            self.bridge_copy().wait_recv()
+
+        value = self.half_sum[...].astype(f32)
+        for slot in range(half, far_count):
             value = value + self.far_in[slot].astype(f32)
         self.total[self.own, :] = value.astype(bf16)
         rows = self.total.at[self.own]
@@ -109,8 +157,18 @@
             copy.wait_recv()
 
     def close(self):
+        place = self.place
         for copy in self.copies:
             copy.wait_send()
+        for step in far_steps:
+
+            @pl.when((place.pair >= half) | (place.far_pair(step) < half))
+            def _(step=step):
+                self.far_copy(step).wait_send()
+
+        @pl.when(place.pair < half)
+        def _():
+            self.bridge_copy().wait_send()
 
 
 def column_picks(column, count):
@@ -238,15 +296,16 @@
     rounded,
     near_in,
     far_in,
+    half_sums,
     total,
     load_sems,
     hand_sems,
     sum_sems,
+    greeting,
 ):
     place = Place()
     barrier = pltpu.get_barrier_semaphore()
-    greeted = [place.far(step) for step in far_steps]
-    greeted += [place.near(step)[0] for step in near_steps]
+    greeted = [place.near(step)[0] for step in near_steps]
     greeted += [place.next_epoch(), place.last_epoch()]
     loads = [
         pltpu.make_async_copy(stored, held, load_sems.at[slot])
@@ -267,6 +326,12 @@
     ]
     for load in loads[:8]:
         load.start()
+    for step in far_steps:
+
+        @pl.when((place.pair < half) | (place.far_pair(step) >= half))
+        def _(step=step):
+            pl.semaphore_signal(barrier, 1, device_id=place.far(step), device_id_type=MESH)
+
     for device in greeted:
         pl.semaphore_signal(barrier, 1, device_id=device, device_id_type=MESH)
     for load in loads[:8]:
@@ -287,7 +352,12 @@
     link_gradient(
         stacked, master[...].astype(bf16), logits_out, 0, deltas, gradient, rounded.at[0]
     )
-    pl.semaphore_wait(barrier, len(greeted))
+    pl.semaphore_wait(barrier, len(greeted) + half - 1 + half * (place.pair // half))
+
+    @pl.when(place.pair >= half)
+    def _():
+        pl.semaphore_signal(greeting, 1, device_id=place.mirror(), device_id_type=MESH)
+
 
     hands = []
     for slot, (kept, handed) in enumerate(
@@ -310,6 +380,7 @@
             rounded.at[batch],
             near_in.at[batch],
             far_in.at[batch],
+            half_sums.at[batch],
             (total, last_total)[batch],
             sum_sems.at[batch],
         )
@@ -334,6 +405,7 @@
     gather_events(
         handed_memory, second_columns, near_id_table, near_time_table, stacked, target_rows
     )
+    sums[0].bridge(greeting)
     sums[0].gather()
     sums[0].arrive()
 
@@ -346,6 +418,7 @@
     fresh = fresh_rows(stacked[0:events, :], target_rows[...], gru_input, gru_state)
     sums[1].exchange()
     memory_out[...] = replaced(handed_memory, ids[3:4, :], fresh)
+    sums[1].bridge(None)
     sums[1].gather()
     sums[1].arrive()
     for hand in hands:
@@ -407,10 +480,12 @@
             vmem((batches, hidden, width), bf16),
             vmem((batches, near_count, hidden // near_count, width), bf16),
             vmem((batches, far_count, hidden // near_count, width), bf16),
+            vmem((batches, hidden // near_count, width), bf16),
             vmem((hidden, width), bf16),
             dma((10,)),
             dma((2, 2)),
             dma((batches, 6, near_count)),
+            pltpu.SemaphoreType.REGULAR,
         ],
         compiler_params=pltpu.CompilerParams(
             collective_id=0, has_side_effects=True, vmem_limit_bytes=50 * 2**20

time: 60.8 us -> 59.1 us (0.972)
  Pallas kernels: 60 us -> 58.3 us
    pallas_call x1, Pallas kernels: 58.7 us -> 57 us  [on_device(): pl.pallas_call(window_kernel, out_shape=(vmem((nodes, width), bf16), vmem...]
where the time goes in v5:
time: 59.1 us; the launch traced here: 59 us
  Pallas kernels  58.3 us (99%)
  between operations  0.64 us (1%)
    pallas_call x1, Pallas kernels, on_device(): pl.pallas_call(window_kernel, out_shape=(vmem((nodes, width), bf16), vmem...  57 us
    pallas_call x1, Pallas kernels, on_device(): pl.pallas_call(results_kernel, out_shape=(jax.ShapeDtypeStruct((1, nodes,...  1.32 us

profile of v5, /device:TPU:1, one launch (start us, length us, event | category | flops | bytes accessed | tf_op | source)
XLA Modules:
  0.0 59.0 jit_solution(1968701969768628684)
XLA Ops:
  0.6 57.0 %window.1 = (bf16[512,512]{1,0:T(8,128)(2,1)S(1)}, f32[256,512]{1,0:T(8,128)S(1)}, bf16[256,512]{1,0:T(8,128)(2,1)S(1)}, f32[4,256]{1,0:T(4,128)S(1)}) custom-call(bf16[512,512]{1,0:T(8,128)(2,1)} %memory_hbm.1, s32[10,512]{1,0:T(8,128)} %near_ids_hbm.1, s32[10,512]{1,0:T(8,128)} %near_times_hbm.1, s32[1,2,256]{2,1,0:T(2,128)} %source_ids_hbm.1, ...), custom_call_target="tpu_custom_call" | custom-call | tf_op jit(solution)/shard_map/window/pallas_call | solution.py:452
  57.6 1.3 %results.1 = (bf16[1,512,512]{2,1,0:T(8,128)(2,1)}, f32[1,512,256]{2,1,0:T(8,128)}, f32[1,4,256]{2,1,0:T(4,128)}) custom-call(bf16[512,512]{1,0:T(8,128)(2,1)S(1)} %get-tuple-element.7.memory, f32[256,512]{1,0:T(8,128)S(1)} %get-tuple-element.8.master, bf16[256,512]{1,0:T(8,128)(2,1)S(1)} %get-tuple-element.9.total, f32[4,256]{1,0:T(4,128)S(1)} %get-tuple-element.10.logits), custom_call_target="tpu_custom_call" | custom-call | tf_op jit(solution)/shard_map/results/pallas_call | solution.py:496

commit v6 on v5

--- a/solution.py
+++ b/solution.py
@@ -61,10 +61,15 @@
 
 
 class TrainerSum:
-    def __init__(self, place, gradient, rounded, near_in, far_in, half_sum, total, sems):
+    def __init__(
+        self, place, gradient, rounded, near_in, far_in, half_sum, total, sems, greetings, chain
+    ):
         self.place, self.gradient, self.rounded = place, gradient, rounded
         self.near_in, self.far_in, self.half_sum = near_in, far_in, half_sum
-        self.total, self.sems = total, sems
+        self.total, self.sems, self.greetings = total, sems, greetings
+        self.chained = chain is not None
+        if self.chained:
+            self.chain_in, self.chain_out, self.running = (chain.at[slot] for slot in range(3))
         self.own = pl.ds(pl.multiple_of(place.piece * 16, 16), 16)
         self.copies = []
 
@@ -99,11 +104,22 @@
             value = value + self.near_in[step].astype(f32)
         place = self.place
         self.far_in[place.pair] = value.astype(bf16)
+        if not self.chained:
+            for step in range(2, half):
+
+                @pl.when(place.pair + step < half)
+                def _(step=step):
+                    pl.semaphore_wait(self.greetings.at[step], 1)
+
         for step in far_steps:
 
-            @pl.when((place.pair >= half) | (place.far_pair(step) < half))
+            @pl.when(self.sends_far(step))
             def _(step=step):
                 self.far_copy(step).start()
+
+    def sends_far(self, step):
+        pair, peer = self.place.pair, self.place.far_pair(step)
+        return (pair >= half) | (peer < (pair if self.chained else half))
 
     def far_copy(self, step):
         slot = self.far_in.at[self.place.pair]
@@ -112,24 +128,54 @@
     def bridge_copy(self):
         return self.copy_of(self.half_sum, self.half_sum, 1, 0, self.place.mirror())
 
-    def bridge(self, greeting):
+    def chain_copy(self):
+        return self.copy_of(self.chain_out, self.chain_in, 2, 0, self.place.far(1))
+
+    def bridge(self):
         place = self.place
 
         @pl.when(place.pair < half)
         def _():
-            for step in far_steps:
-
-                @pl.when(place.far_pair(-step) < half)
-                def _(step=step):
-                    self.far_copy(step).wait_recv()
-
-            value = self.far_in[0].astype(f32)
-            for slot in range(1, half):
-                value = value + self.far_in[slot].astype(f32)
-            self.half_sum[...] = value.astype(bf16)
-            if greeting is not None:
-                pl.semaphore_wait(greeting, 1)
+            if self.chained:
+                self.chain_out[...] = self.far_in[place.pair].astype(f32)
+
+                @pl.when(place.pair > 0)
+                def _():
+                    self.chain_copy().wait_recv()
+                    self.chain_out[...] += self.chain_in[...]
+
+                @pl.when(place.pair < half - 1)
+                def _():
+                    pl.semaphore_wait(self.greetings.at[1], 1)
+                    self.chain_copy().start()
+
+                self.running[...] = self.chain_out[...]
+                for pair in range(1, half):
+
+                    @pl.when(place.pair < pair)
+                    def _(pair=pair):
+                        self.arrived_from(pair)
+                        self.running[...] += self.far_in[pair].astype(f32)
+
+                self.half_sum[...] = self.running[...].astype(bf16)
+                pl.semaphore_wait(self.greetings.at[0], 1)
+            else:
+                for step in far_steps:
+
+                    @pl.when(place.far_pair(-step) < half)
+                    def _(step=step):
+                        self.far_copy(step).wait_recv()
+
+                value = self.far_in[0].astype(f32)
+                for slot in range(1, half):
+                    value = value + self.far_in[slot].astype(f32)
+                self.half_sum[...] = value.astype(bf16)
             self.bridge_copy().start()
+
+    def arrived_from(self, pair):
+        step = (self.place.pair - pair + far_count) % far_count
+        slot = self.far_in.at[pair]
+        self.copy_of(slot, slot, 1, step, self.place.far(1)).wait_recv()
 
     def gather(self):
         place = self.place
@@ -162,13 +208,19 @@
             copy.wait_send()
         for step in far_steps:
 
-            @pl.when((place.pair >= half) | (place.far_pair(step) < half))
+            @pl.when(self.sends_far(step))
             def _(step=step):
                 self.far_copy(step).wait_send()
 
         @pl.when(place.pair < half)
         def _():
             self.bridge_copy().wait_send()
+
+        if self.chained:
+
+            @pl.when(place.pair < half - 1)
+            def _():
+                self.chain_copy().wait_send()
 
 
 def column_picks(column, count):
@@ -297,11 +349,12 @@
     near_in,
     far_in,
     half_sums,
+    chain,
     total,
     load_sems,
     hand_sems,
     sum_sems,
-    greeting,
+    greetings,
 ):
     place = Place()
     barrier = pltpu.get_barrier_semaphore()
@@ -328,7 +381,10 @@
         load.start()
     for step in far_steps:
 
-        @pl.when((place.pair < half) | (place.far_pair(step) >= half))
+        @pl.when(
+            (place.far_pair(step) > place.pair)
+            | ((place.pair >= half) & (place.far_pair(step) >= half))
+        )
         def _(step=step):
             pl.semaphore_signal(barrier, 1, device_id=place.far(step), device_id_type=MESH)
 
@@ -352,11 +408,21 @@
     link_gradient(
         stacked, master[...].astype(bf16), logits_out, 0, deltas, gradient, rounded.at[0]
     )
-    pl.semaphore_wait(barrier, len(greeted) + half - 1 + half * (place.pair // half))
+    late = place.pair // half
+    earlier = (1 - late) * place.pair + late * (far_count - 1)
+    pl.semaphore_wait(barrier, len(greeted) + earlier)
 
     @pl.when(place.pair >= half)
     def _():
-        pl.semaphore_signal(greeting, 1, device_id=place.mirror(), device_id_type=MESH)
+        pl.semaphore_signal(greetings.at[0], 1, device_id=place.mirror(), device_id_type=MESH)
+
+    for step in range(1, half):
+
+        @pl.when((place.pair < half) & (place.pair >= step))
+        def _(step=step):
+            pl.semaphore_signal(
+                greetings.at[step], 1, device_id=place.far(-step), device_id_type=MESH
+            )
 
 
     hands = []
@@ -383,6 +449,8 @@
             half_sums.at[batch],
             (total, last_total)[batch],
             sum_sems.at[batch],
+            greetings,
+            (chain, None)[batch],
         )
         for batch in range(2)
     ]
@@ -405,7 +473,7 @@
     gather_events(
         handed_memory, second_columns, near_id_table, near_time_table, stacked, target_rows
     )
-    sums[0].bridge(greeting)
+    sums[0].bridge()
     sums[0].gather()
     sums[0].arrive()
 
@@ -418,7 +486,7 @@
     fresh = fresh_rows(stacked[0:events, :], target_rows[...], gru_input, gru_state)
     sums[1].exchange()
     memory_out[...] = replaced(handed_memory, ids[3:4, :], fresh)
-    sums[1].bridge(None)
+    sums[1].bridge()
     sums[1].gather()
     sums[1].arrive()
     for hand in hands:
@@ -481,11 +549,12 @@
             vmem((batches, near_count, hidden // near_count, width), bf16),
             vmem((batches, far_count, hidden // near_count, width), bf16),
             vmem((batches, hidden // near_count, width), bf16),
+            vmem((3, hidden // near_count, width), f32),
             vmem((hidden, width), bf16),
             dma((10,)),
             dma((2, 2)),
             dma((batches, 6, near_count)),
-            pltpu.SemaphoreType.REGULAR,
+            pltpu.SemaphoreType.REGULAR((half,)),
         ],
         compiler_params=pltpu.CompilerParams(
             collective_id=0, has_side_effects=True, vmem_limit_bytes=50 * 2**20

time: 59.1 us -> 61.5 us (1.041)
  Pallas kernels: 58.3 us -> 60.7 us
    pallas_call x1, Pallas kernels: 57 us -> 59.4 us  [on_device(): pl.pallas_call(window_kernel, out_shape=(vmem((nodes, width), bf16), vmem...]
where the time goes in v6:
time: 61.5 us; the launch traced here: 61.3 us
  Pallas kernels  60.7 us (99%)
  between operations  0.64 us (1%)
    pallas_call x1, Pallas kernels, on_device(): pl.pallas_call(window_kernel, out_shape=(vmem((nodes, width), bf16), vmem...  59.4 us
    pallas_call x1, Pallas kernels, on_device(): pl.pallas_call(results_kernel, out_shape=(jax.ShapeDtypeStruct((1, nodes,...  1.32 us

profile of v6, /device:TPU:1, one launch (start us, length us, event | category | flops | bytes accessed | tf_op | source)
XLA Modules:
  0.0 61.3 jit_solution(13630279742452534812)
XLA Ops:
  0.6 59.4 %window.1 = (bf16[512,512]{1,0:T(8,128)(2,1)S(1)}, f32[256,512]{1,0:T(8,128)S(1)}, bf16[256,512]{1,0:T(8,128)(2,1)S(1)}, f32[4,256]{1,0:T(4,128)S(1)}) custom-call(bf16[512,512]{1,0:T(8,128)(2,1)} %memory_hbm.1, s32[10,512]{1,0:T(8,128)} %near_ids_hbm.1, s32[10,512]{1,0:T(8,128)} %near_times_hbm.1, s32[1,2,256]{2,1,0:T(2,128)} %source_ids_hbm.1, ...), custom_call_target="tpu_custom_call" | custom-call | tf_op jit(solution)/shard_map/window/pallas_call | solution.py:520
  60.0 1.3 %results.1 = (bf16[1,512,512]{2,1,0:T(8,128)(2,1)}, f32[1,512,256]{2,1,0:T(8,128)}, f32[1,4,256]{2,1,0:T(4,128)}) custom-call(bf16[512,512]{1,0:T(8,128)(2,1)S(1)} %get-tuple-element.7.memory, f32[256,512]{1,0:T(8,128)S(1)} %get-tuple-element.8.master, bf16[256,512]{1,0:T(8,128)(2,1)S(1)} %get-tuple-element.9.total, f32[4,256]{1,0:T(4,128)S(1)} %get-tuple-element.10.logits), custom_call_target="tpu_custom_call" | custom-call | tf_op jit(solution)/shard_map/results/pallas_call | solution.py:565

commit v7 on v5

--- a/solution.py
+++ b/solution.py
@@ -12,6 +12,7 @@
 epsilon = 1e-06
 near_count, far_count = 16, 8
 half = far_count // 2
+near_out, early_out, late_out, bridge_out, back_out = range(5)
 
 
 def matmul(a, b):
@@ -66,63 +67,51 @@
         self.near_in, self.far_in, self.half_sum = near_in, far_in, half_sum
         self.total, self.sems = total, sems
         self.own = pl.ds(pl.multiple_of(place.piece * 16, 16), 16)
-        self.copies = []
-
-    def copy_of(self, src, dst, stage, step, device):
+
+    def copy_of(self, src, dst, stage, device):
         return pltpu.make_async_remote_copy(
             src_ref=src,
             dst_ref=dst,
-            send_sem=self.sems.at[2 * stage, step],
-            recv_sem=self.sems.at[2 * stage + 1, step],
+            send_sem=self.sems.at[0, stage],
+            recv_sem=self.sems.at[1, stage],
             device_id=device,
             device_id_type=MESH,
         )
 
-    def send(self, src, dst, stage, step, device):
-        copy = self.copy_of(src, dst, stage, step, device)
-        copy.start()
-        self.copies.append(copy)
-        return copy
+    def all_of(self, rows, stage):
+        return self.copy_of(rows, rows, stage, self.place.mirror())
 
     def scatter(self):
-        self.pending = []
         for step in near_steps:
             device, piece = self.place.near(step)
             rows = pl.ds(pl.multiple_of(piece * 16, 16), 16)
-            copy = self.send(self.rounded.at[rows], self.near_in.at[step], 0, step, device)
-            self.pending.append((step, copy))
+            self.copy_of(self.rounded.at[rows], self.near_in.at[step - 1], near_out, device).start()
 
     def exchange(self):
+        self.all_of(self.near_in, near_out).wait_recv()
         value = self.gradient[self.own, :]
-        for step, copy in reversed(self.pending):
-            copy.wait_recv()
-            value = value + self.near_in[step].astype(f32)
+        for slot in range(near_count - 1):
+            value = value + self.near_in[slot].astype(f32)
         place = self.place
         self.far_in[place.pair] = value.astype(bf16)
+        slot = self.far_in.at[place.pair]
         for step in far_steps:
 
-            @pl.when((place.pair >= half) | (place.far_pair(step) < half))
+            @pl.when(place.pair >= half)
             def _(step=step):
-                self.far_copy(step).start()
-
-    def far_copy(self, step):
-        slot = self.far_in.at[self.place.pair]
-        return self.copy_of(slot, slot, 1, step, self.place.far(step))
+                self.copy_of(slot, slot, late_out, place.far(step)).start()
+
+            @pl.when((place.pair < half) & (place.far_pair(step) < half))
+            def _(step=step):
+                self.copy_of(slot, slot, early_out, place.far(step)).start()
 
     def bridge_copy(self):
-        return self.copy_of(self.half_sum, self.half_sum, 1, 0, self.place.mirror())
+        return self.copy_of(self.half_sum, self.half_sum, bridge_out, self.place.mirror())
 
     def bridge(self, greeting):
-        place = self.place
-
-        @pl.when(place.pair < half)
+        @pl.when(self.place.pair < half)
         def _():
-            for step in far_steps:
-
-                @pl.when(place.far_pair(-step) < half)
-                def _(step=step):
-                    self.far_copy(step).wait_recv()
-
+            self.all_of(self.far_in.at[: half - 1], early_out).wait_recv()
             value = self.far_in[0].astype(f32)
             for slot in range(1, half):
                 value = value + self.far_in[slot].astype(f32)
@@ -132,15 +121,13 @@
             self.bridge_copy().start()
 
     def gather(self):
-        place = self.place
-        for step in far_steps:
-
-            @pl.when(place.far_pair(-step) >= half)
-            def _(step=step):
-                self.far_copy(step).wait_recv()
-
-        @pl.when(place.pair >= half)
+        @pl.when(self.place.pair < half)
         def _():
+            self.all_of(self.far_in.at[:half], late_out).wait_recv()
+
+        @pl.when(self.place.pair >= half)
+        def _():
+            self.all_of(self.far_in.at[: half - 1], late_out).wait_recv()
             self.bridge_copy().wait_recv()
 
         value = self.half_sum[...].astype(f32)
@@ -148,27 +135,24 @@
             value = value + self.far_in[slot].astype(f32)
         self.total[self.own, :] = value.astype(bf16)
         rows = self.total.at[self.own]
-        self.pending = [
-            self.send(rows, rows, 2, step, self.place.near(step)[0]) for step in near_steps
-        ]
+        for step in near_steps:
+            self.copy_of(rows, rows, back_out, self.place.near(step)[0]).start()
 
     def arrive(self):
-        for copy in self.pending:
-            copy.wait_recv()
+        self.all_of(self.near_in, back_out).wait_recv()
 
     def close(self):
-        place = self.place
-        for copy in self.copies:
-            copy.wait_send()
-        for step in far_steps:
-
-            @pl.when((place.pair >= half) | (place.far_pair(step) < half))
-            def _(step=step):
-                self.far_copy(step).wait_send()
-
-        @pl.when(place.pair < half)
+        self.all_of(self.near_in, near_out).wait_send()
+        self.all_of(self.near_in, back_out).wait_send()
+
+        @pl.when(self.place.pair < half)
         def _():
+            self.all_of(self.far_in.at[: half - 1], early_out).wait_send()
             self.bridge_copy().wait_send()
+
+        @pl.when(self.place.pair >= half)
+        def _():
+            self.all_of(self.far_in.at[: far_count - 1], late_out).wait_send()
 
 
 def column_picks(column, count):
@@ -199,18 +183,20 @@
     return weights
 
 
-def gather_events(memory, columns, near_ids, near_times, stacked, target_rows):
+def gather_events(memory, columns, near_ids, near_times, picks, stacked, target_rows):
     source, target, negative, ticks = columns
     events, nodes = source.shape[0], memory.shape[0]
     target_picks = column_picks(target, nodes)
-    stacked[0:events, :] = matmul(column_picks(source, nodes), memory[...]).astype(bf16)
-    stacked[2 * events :, :] = matmul(column_picks(negative, nodes), memory[...]).astype(bf16)
-    rows = matmul(target_picks, memory[...])
+    picks[0:events, :] = column_picks(source, nodes)
+    picks[events : 2 * events, :] = column_picks(negative, nodes)
+    picks[2 * events :, :] = target_picks
+    rows = matmul(picks[...], memory[...])
+    stacked[0:events, :] = rows[0:events].astype(bf16)
+    stacked[2 * events :, :] = rows[events : 2 * events].astype(bf16)
+    rows = rows[2 * events :]
     target_rows[...] = rows.astype(bf16)
     weights = neighbour_weights(target_picks, ticks, near_ids, near_times)
-    high = weights.astype(bf16)
-    low = (weights - high.astype(f32)).astype(bf16)
-    aggregate = matmul(high, memory[...]) + matmul(low, memory[...])
+    aggregate = matmul(weights.astype(bf16), memory[...])
     stacked[events : 2 * events, :] = (0.5 * (rows + aggregate)).astype(bf16)
 
 
@@ -289,6 +275,7 @@
     handed_source,
     handed_target,
     handed_memory,
+    picks,
     stacked,
     target_rows,
     deltas,
@@ -348,7 +335,9 @@
     master[...] = decoder[...].astype(f32).T
     near_id_table, near_time_table = near_ids[...], near_times[...]
 
-    gather_events(memory, first_columns, near_id_table, near_time_table, stacked, target_rows)
+    gather_events(
+        memory, first_columns, near_id_table, near_time_table, picks, stacked, target_rows
+    )
     link_gradient(
         stacked, master[...].astype(bf16), logits_out, 0, deltas, gradient, rounded.at[0]
     )
@@ -403,7 +392,7 @@
 
     handed_memory[...] = replaced(memory, handed_rows[2:3, :], fresh)
     gather_events(
-        handed_memory, second_columns, near_id_table, near_time_table, stacked, target_rows
+        handed_memory, second_columns, near_id_table, near_time_table, picks, stacked, target_rows
     )
     sums[0].bridge(greeting)
     sums[0].gather()
@@ -473,18 +462,19 @@
             vmem((batches, events), jnp.int32),
             vmem((batches, events), jnp.int32),
             vmem((nodes, width), bf16),
+            vmem((3 * events, nodes), bf16),
             vmem((3 * events, width), bf16),
             vmem((events, width), bf16),
             vmem((hidden, 3 * events), bf16),
             vmem((hidden, width), f32),
             vmem((batches, hidden, width), bf16),
-            vmem((batches, near_count, hidden // near_count, width), bf16),
+            vmem((batches, near_count - 1, hidden // near_count, width), bf16),
             vmem((batches, far_count, hidden // near_count, width), bf16),
             vmem((batches, hidden // near_count, width), bf16),
             vmem((hidden, width), bf16),
             dma((10,)),
             dma((2, 2)),
-            dma((batches, 6, near_count)),
+            dma((batches, 2, 5)),
             pltpu.SemaphoreType.REGULAR,
         ],
         compiler_params=pltpu.CompilerParams(

time: 59.1 us -> 57.2 us (0.968)
  Pallas kernels: 58.3 us -> 56.4 us
    pallas_call x1, Pallas kernels: 57 us -> 55.1 us  [on_device(): pl.pallas_call(window_kernel, out_shape=(vmem((nodes, width), bf16), vmem...]
where the time goes in v7:
time: 57.2 us; the launch traced here: 57.1 us
  Pallas kernels  56.4 us (99%)
  between operations  0.64 us (1%)
    pallas_call x1, Pallas kernels, on_device(): pl.pallas_call(window_kernel, out_shape=(vmem((nodes, width), bf16), vmem...  55.1 us
    pallas_call x1, Pallas kernels, on_device(): pl.pallas_call(results_kernel, out_shape=(jax.ShapeDtypeStruct((1, nodes,...  1.32 us

profile of v7, /device:TPU:1, one launch (start us, length us, event | category | flops | bytes accessed | tf_op | source)
XLA Modules:
  0.0 57.1 jit_solution(2808049507252909003)
XLA Ops:
  0.6 55.1 %window.1 = (bf16[512,512]{1,0:T(8,128)(2,1)S(1)}, f32[256,512]{1,0:T(8,128)S(1)}, bf16[256,512]{1,0:T(8,128)(2,1)S(1)}, f32[4,256]{1,0:T(4,128)S(1)}) custom-call(bf16[512,512]{1,0:T(8,128)(2,1)} %memory_hbm.1, s32[10,512]{1,0:T(8,128)} %near_ids_hbm.1, s32[10,512]{1,0:T(8,128)} %near_times_hbm.1, s32[1,2,256]{2,1,0:T(2,128)} %source_ids_hbm.1, ...), custom_call_target="tpu_custom_call" | custom-call | tf_op jit(solution)/shard_map/window/pallas_call | solution.py:441
  55.8 1.3 %results.1 = (bf16[1,512,512]{2,1,0:T(8,128)(2,1)}, f32[1,512,256]{2,1,0:T(8,128)}, f32[1,4,256]{2,1,0:T(4,128)}) custom-call(bf16[512,512]{1,0:T(8,128)(2,1)S(1)} %get-tuple-element.7.memory, f32[256,512]{1,0:T(8,128)S(1)} %get-tuple-element.8.master, bf16[256,512]{1,0:T(8,128)(2,1)S(1)} %get-tuple-element.9.total, f32[4,256]{1,0:T(4,128)S(1)} %get-tuple-element.10.logits), custom_call_target="tpu_custom_call" | custom-call | tf_op jit(solution)/shard_map/results/pallas_call | solution.py:486

commit v8 on v7

--- a/solution.py
+++ b/solution.py
@@ -165,38 +165,44 @@
     return jnp.where(row == names, 1.0, 0.0)
 
 
-def neighbour_weights(target_picks, ticks, near_ids, near_times):
-    def looked_up(table):
-        low = (table & 255).astype(f32).astype(bf16)
-        high = (table >> 8).astype(f32).astype(bf16)
-        return matmul_nt(target_picks, low) + 256.0 * matmul_nt(target_picks, high)
-
-    ids, times = looked_up(near_ids), looked_up(near_times)
+def fill_table(table, near_ids, near_times):
+    table[...] = jnp.zeros_like(table)
+    count = near_ids.shape[0]
+    for part, value in enumerate((near_ids, near_ids, near_times, near_times)):
+        value = value[...] >> 8 if part % 2 else value[...] & 255
+        table[16 * part : 16 * part + count, :] = value.astype(f32).astype(bf16)
+
+
+def neighbour_weights(found, count, ticks, nodes):
+    ids = found[:, 0:count] + 256.0 * found[:, 16 : 16 + count]
+    times = found[:, 32 : 32 + count] + 256.0 * found[:, 48 : 48 + count]
     decay = tick_scale / (tick_scale + (ticks - times))
     decay = decay / jnp.sum(decay, axis=1, keepdims=True)
-    events, nodes = target_picks.shape
+    events = found.shape[0]
     lanes = lax.broadcasted_iota(jnp.int32, (events, nodes), 1).astype(f32)
     weights = jnp.zeros((events, nodes), f32)
-    for slot in range(near_ids.shape[0]):
+    for slot in range(count):
         chosen = ids[:, slot : slot + 1] == lanes
         weights = weights + jnp.where(chosen, decay[:, slot : slot + 1], 0.0)
     return weights
 
 
-def gather_events(memory, columns, near_ids, near_times, picks, stacked, target_rows):
+def gather_events(memory, columns, table, count, picks, stacked, target_rows, ready):
     source, target, negative, ticks = columns
     events, nodes = source.shape[0], memory.shape[0]
     target_picks = column_picks(target, nodes)
+    found = matmul_nt(target_picks, table[...])
+    picks[2 * events :, :] = target_picks
     picks[0:events, :] = column_picks(source, nodes)
     picks[events : 2 * events, :] = column_picks(negative, nodes)
-    picks[2 * events :, :] = target_picks
+    ready()
     rows = matmul(picks[...], memory[...])
+    weights = neighbour_weights(found, count, ticks, nodes).astype(bf16)
     stacked[0:events, :] = rows[0:events].astype(bf16)
     stacked[2 * events :, :] = rows[events : 2 * events].astype(bf16)
     rows = rows[2 * events :]
     target_rows[...] = rows.astype(bf16)
-    weights = neighbour_weights(target_picks, ticks, near_ids, near_times)
-    aggregate = matmul(weights.astype(bf16), memory[...])
+    aggregate = matmul(weights, memory[...])
     stacked[events : 2 * events, :] = (0.5 * (rows + aggregate)).astype(bf16)
 
 
@@ -242,9 +248,13 @@
     return jnp.where(hit > 0.5, placed, memory[...].astype(f32)).astype(bf16)
 
 
-def stepped(master, total):
+def step_scale(total):
     total = total[...].astype(f32)
-    return master - step_length * total / jnp.sqrt(jnp.sum(total * total) + epsilon)
+    return step_length / jnp.sqrt(jnp.sum(total * total) + epsilon)
+
+
+def stepped(master, total, scale):
+    return master - scale * total.astype(f32)
 
 
 def window_kernel(
@@ -275,6 +285,7 @@
     handed_source,
     handed_target,
     handed_memory,
+    table,
     picks,
     stacked,
     target_rows,
@@ -298,13 +309,13 @@
         pltpu.make_async_copy(stored, held, load_sems.at[slot])
         for slot, (stored, held) in enumerate(
             (
-                (memory_hbm, memory),
                 (source_ids_hbm, source_ids),
                 (target_ids_hbm, target_ids),
                 (negative_ids_hbm, negative_ids),
                 (event_ticks_hbm, event_ticks),
                 (near_ids_hbm, near_ids),
                 (near_times_hbm, near_times),
+                (memory_hbm, memory),
                 (decoder_hbm, decoder),
                 (gru_input_hbm, gru_input),
                 (gru_state_hbm, gru_state),
@@ -321,10 +332,8 @@
 
     for device in greeted:
         pl.semaphore_signal(barrier, 1, device_id=device, device_id_type=MESH)
-    for load in loads[:8]:
+    for load in loads[:6]:
         load.wait()
-    for load in loads[8:]:
-        load.start()
 
     ids = jnp.concatenate(
         [source_ids[0], target_ids[0], negative_ids[0], event_ticks[0]], axis=0
@@ -332,12 +341,17 @@
     columns = ids.T
     first_columns = [columns[:, 2 * kind : 2 * kind + 1] for kind in range(4)]
     second_columns = [columns[:, 2 * kind + 1 : 2 * kind + 2] for kind in range(4)]
-    master[...] = decoder[...].astype(f32).T
-    near_id_table, near_time_table = near_ids[...], near_times[...]
-
-    gather_events(
-        memory, first_columns, near_id_table, near_time_table, picks, stacked, target_rows
-    )
+    fill_table(table, near_ids, near_times)
+    count = near_ids.shape[0]
+
+    def loaded():
+        for load in loads[6:8]:
+            load.wait()
+        for load in loads[8:]:
+            load.start()
+        master[...] = decoder[...].astype(f32).T
+
+    gather_events(memory, first_columns, table, count, picks, stacked, target_rows, loaded)
     link_gradient(
         stacked, master[...].astype(bf16), logits_out, 0, deltas, gradient, rounded.at[0]
     )
@@ -392,13 +406,13 @@
 
     handed_memory[...] = replaced(memory, handed_rows[2:3, :], fresh)
     gather_events(
-        handed_memory, second_columns, near_id_table, near_time_table, picks, stacked, target_rows
+        handed_memory, second_columns, table, count, picks, stacked, target_rows, lambda: None
     )
     sums[0].bridge(greeting)
     sums[0].gather()
     sums[0].arrive()
 
-    master[...] = stepped(master[...], total)
+    master[...] = stepped(master[...], total[...], step_scale(total))
     link_gradient(
         stacked, master[...].astype(bf16), logits_out, 2, deltas, gradient, rounded.at[1]
     )
@@ -420,12 +434,20 @@
     stores = [
         pltpu.make_async_copy(memory, memory_out.at[0], sems.at[0]),
         pltpu.make_async_copy(logits, logits_out.at[0], sems.at[1]),
-        pltpu.make_async_copy(decoder, decoder_out.at[0], sems.at[2]),
     ]
-    stores[0].start()
-    stores[1].start()
-    decoder[...] = stepped(master[...], total).T
-    stores[2].start()
+    for store in stores:
+        store.start()
+    scale = step_scale(total)
+    parts = decoder.shape[0] // 128
+    for part in range(parts):
+        rows = slice(128 * part, 128 * (part + 1))
+        decoder[rows, :] = stepped(master[:, rows], total[:, rows], scale).T
+        stores.append(
+            pltpu.make_async_copy(
+                decoder.at[rows], decoder_out.at[0, rows], sems.at[2 + part]
+            )
+        )
+        stores[-1].start()
     for store in stores:
         store.wait()
 
@@ -462,6 +484,7 @@
             vmem((batches, events), jnp.int32),
             vmem((batches, events), jnp.int32),
             vmem((nodes, width), bf16),
+            vmem((64, nodes), bf16),
             vmem((3 * events, nodes), bf16),
             vmem((3 * events, width), bf16),
             vmem((events, width), bf16),
@@ -492,7 +515,7 @@
         ),
         in_specs=[held] * 4,
         out_specs=(stored,) * 3,
-        scratch_shapes=[vmem((width, hidden), f32), dma((3,))],
+        scratch_shapes=[vmem((width, hidden), f32), dma((2 + width // 128,))],
         compiler_params=pltpu.CompilerParams(vmem_limit_bytes=8 * 2**20),
         name="results",
     )(*(pltpu.with_memory_space_constraint(each, pltpu.VMEM) for each in kept))

time: 57.2 us -> 57 us (level)
  no operation moved by 1% of the time
where the time goes in v8:
time: 57 us; the launch traced here: 56.9 us
  Pallas kernels  56.3 us (99%)
  between operations  0.64 us (1%)
    pallas_call x1, Pallas kernels, on_device(): pl.pallas_call(window_kernel, out_shape=(vmem((nodes, width), bf16), vmem...  55 us
    pallas_call x1, Pallas kernels, on_device(): pl.pallas_call(results_kernel, out_shape=(jax.ShapeDtypeStruct((1, nodes,...  1.27 us

profile of v8, /device:TPU:1, one launch (start us, length us, event | category | flops | bytes accessed | tf_op | source)
XLA Modules:
  0.0 56.9 jit_solution(17815933850331296627)
XLA Ops:
  0.6 55.0 %window.1 = (bf16[512,512]{1,0:T(8,128)(2,1)S(1)}, f32[256,512]{1,0:T(8,128)S(1)}, bf16[256,512]{1,0:T(8,128)(2,1)S(1)}, f32[4,256]{1,0:T(4,128)S(1)}) custom-call(bf16[512,512]{1,0:T(8,128)(2,1)} %memory_hbm.1, s32[10,512]{1,0:T(8,128)} %near_ids_hbm.1, s32[10,512]{1,0:T(8,128)} %near_times_hbm.1, s32[1,2,256]{2,1,0:T(2,128)} %source_ids_hbm.1, ...), custom_call_target="tpu_custom_call" | custom-call | tf_op jit(solution)/shard_map/window/pallas_call | solution.py:463
  55.6 1.3 %results.1 = (bf16[1,512,512]{2,1,0:T(8,128)(2,1)}, f32[1,512,256]{2,1,0:T(8,128)}, f32[1,4,256]{2,1,0:T(4,128)}) custom-call(bf16[512,512]{1,0:T(8,128)(2,1)S(1)} %get-tuple-element.7.memory, f32[256,512]{1,0:T(8,128)S(1)} %get-tuple-element.8.master, bf16[256,512]{1,0:T(8,128)(2,1)S(1)} %get-tuple-element.9.total, f32[4,256]{1,0:T(4,128)S(1)} %get-tuple-element.10.logits), custom_call_target="tpu_custom_call" | custom-call | tf_op jit(solution)/shard_map/results/pallas_call | solution.py:509

commit v9 on v8

--- a/solution.py
+++ b/solution.py
@@ -44,11 +44,14 @@
     def far_pair(self, step):
         return (self.pair + step + far_count) % far_count
 
+    def at_pair(self, pair):
+        return device_at(self.y, pair * 2 + self.side, self.core)
+
     def far(self, step):
-        return device_at(self.y, self.far_pair(step) * 2 + self.side, self.core)
+        return self.at_pair(self.far_pair(step))
 
     def mirror(self):
-        return device_at(self.y, (far_count - 1 - self.pair) * 2 + self.side, self.core)
+        return self.at_pair(far_count - 1 - self.pair)
 
     def next_epoch(self):
         return {"epoch": (self.epoch + 1) % 4}
@@ -87,7 +90,7 @@
             rows = pl.ds(pl.multiple_of(piece * 16, 16), 16)
             self.copy_of(self.rounded.at[rows], self.near_in.at[step - 1], near_out, device).start()
 
-    def exchange(self):
+    def exchange(self, first_pair_first):
         self.all_of(self.near_in, near_out).wait_recv()
         value = self.gradient[self.own, :]
         for slot in range(near_count - 1):
@@ -95,15 +98,19 @@
         place = self.place
         self.far_in[place.pair] = value.astype(bf16)
         slot = self.far_in.at[place.pair]
-        for step in far_steps:
-
-            @pl.when(place.pair >= half)
-            def _(step=step):
-                self.copy_of(slot, slot, late_out, place.far(step)).start()
-
-            @pl.when((place.pair < half) & (place.far_pair(step) < half))
-            def _(step=step):
-                self.copy_of(slot, slot, early_out, place.far(step)).start()
+        if first_pair_first:
+            targets = [(pair, place.at_pair(pair)) for pair in range(far_count)]
+        else:
+            targets = [(place.far_pair(step), place.far(step)) for step in far_steps]
+        for pair, device in targets:
+
+            @pl.when((place.pair >= half) & (place.pair != pair))
+            def _(device=device):
+                self.copy_of(slot, slot, late_out, device).start()
+
+            @pl.when((place.pair < half) & (place.pair != pair) & (pair < half))
+            def _(device=device):
+                self.copy_of(slot, slot, early_out, device).start()
 
     def bridge_copy(self):
         return self.copy_of(self.half_sum, self.half_sum, bridge_out, self.place.mirror())
@@ -402,7 +409,7 @@
     source = matmul(column_picks(handed_columns[:, 0:1], nodes), memory[...]).astype(bf16)
     target = matmul(column_picks(handed_columns[:, 2:3], nodes), memory[...]).astype(bf16)
     fresh = fresh_rows(source, target, gru_input, gru_state)
-    sums[0].exchange()
+    sums[0].exchange(False)
 
     handed_memory[...] = replaced(memory, handed_rows[2:3, :], fresh)
     gather_events(
@@ -419,15 +426,15 @@
     sums[1].scatter()
     events = target_rows.shape[0]
     fresh = fresh_rows(stacked[0:events, :], target_rows[...], gru_input, gru_state)
-    sums[1].exchange()
+    sums[1].exchange(True)
+    sums[0].close()
+    for hand in hands:
+        hand.wait_send()
     memory_out[...] = replaced(handed_memory, ids[3:4, :], fresh)
     sums[1].bridge(None)
     sums[1].gather()
+    sums[1].close()
     sums[1].arrive()
-    for hand in hands:
-        hand.wait_send()
-    for each in sums:
-        each.close()
 
 
 def results_kernel(memory, master, total, logits, memory_out, decoder_out, logits_out, decoder, sems):

time: 57 us -> 57.7 us (1.012)
  Pallas kernels: 56.3 us -> 56.9 us
    pallas_call x1, Pallas kernels: 55 us -> 55.6 us  [on_device(): pl.pallas_call(window_kernel, out_shape=(vmem((nodes, width), bf16), vmem...]
where the time goes in v9:
time: 57.7 us; the launch traced here: 57.5 us
  Pallas kernels  56.9 us (99%)
  between operations  0.64 us (1%)
    pallas_call x1, Pallas kernels, on_device(): pl.pallas_call(window_kernel, out_shape=(vmem((nodes, width), bf16), vmem...  55.6 us
    pallas_call x1, Pallas kernels, on_device(): pl.pallas_call(results_kernel, out_shape=(jax.ShapeDtypeStruct((1, nodes,...  1.27 us

profile of v9, /device:TPU:1, one launch (start us, length us, event | category | flops | bytes accessed | tf_op | source)
XLA Modules:
  0.0 57.5 jit_solution(1680265355399883476)
XLA Ops:
  0.6 55.6 %window.1 = (bf16[512,512]{1,0:T(8,128)(2,1)S(1)}, f32[256,512]{1,0:T(8,128)S(1)}, bf16[256,512]{1,0:T(8,128)(2,1)S(1)}, f32[4,256]{1,0:T(4,128)S(1)}) custom-call(bf16[512,512]{1,0:T(8,128)(2,1)} %memory_hbm.1, s32[10,512]{1,0:T(8,128)} %near_ids_hbm.1, s32[10,512]{1,0:T(8,128)} %near_times_hbm.1, s32[1,2,256]{2,1,0:T(2,128)} %source_ids_hbm.1, ...), custom_call_target="tpu_custom_call" | custom-call | tf_op jit(solution)/shard_map/window/pallas_call | solution.py:470
  56.3 1.3 %results.1 = (bf16[1,512,512]{2,1,0:T(8,128)(2,1)}, f32[1,512,256]{2,1,0:T(8,128)}, f32[1,4,256]{2,1,0:T(4,128)}) custom-call(bf16[512,512]{1,0:T(8,128)(2,1)S(1)} %get-tuple-element.7.memory, f32[256,512]{1,0:T(8,128)S(1)} %get-tuple-element.8.master, bf16[256,512]{1,0:T(8,128)(2,1)S(1)} %get-tuple-element.9.total, f32[4,256]{1,0:T(4,128)S(1)} %get-tuple-element.10.logits), custom_call_target="tpu_custom_call" | custom-call | tf_op jit(solution)/shard_map/results/pallas_call | solution.py:516

commit v10 on v8

--- a/solution.py
+++ b/solution.py
@@ -12,7 +12,9 @@
 epsilon = 1e-06
 near_count, far_count = 16, 8
 half = far_count // 2
-near_out, early_out, late_out, bridge_out, back_out = range(5)
+near_out, early_out, late_out, bridge_out, back_out, relay_out = range(6)
+relayed = (4, 12, 5, 13)
+back_count = near_count - 1 - len(relayed)
 
 
 def matmul(a, b):
@@ -44,11 +46,14 @@
     def far_pair(self, step):
         return (self.pair + step + far_count) % far_count
 
+    def at_pair(self, pair):
+        return device_at(self.y, pair * 2 + self.side, self.core)
+
     def far(self, step):
-        return device_at(self.y, self.far_pair(step) * 2 + self.side, self.core)
+        return self.at_pair(self.far_pair(step))
 
     def mirror(self):
-        return device_at(self.y, (far_count - 1 - self.pair) * 2 + self.side, self.core)
+        return self.at_pair(far_count - 1 - self.pair)
 
     def next_epoch(self):
         return {"epoch": (self.epoch + 1) % 4}
@@ -136,14 +141,30 @@
         self.total[self.own, :] = value.astype(bf16)
         rows = self.total.at[self.own]
         for step in near_steps:
-            self.copy_of(rows, rows, back_out, self.place.near(step)[0]).start()
+            if step in relayed:
+                stage = relay_out + relayed.index(step)
+                self.copy_of(rows, rows, stage, self.place.near(step)[0]).start()
+            elif step // 4 % 2 == 0:
+                self.copy_of(rows, rows, back_out, self.place.near(step)[0]).start()
+
+    def relay(self):
+        place = self.place
+        other = place.near(2)[0]
+        for slot, step in enumerate(relayed):
+            y, side = (place.y - step // 4 + 4) % 4, (place.side + step) % 2
+            start = pl.multiple_of(((y * 2 + place.core) * 2 + side) * 16, 16)
+            rows = self.total.at[pl.ds(start, 16)]
+            self.copy_of(rows, rows, relay_out + slot, other).wait_recv()
+            self.copy_of(rows, rows, back_out, other).start()
 
     def arrive(self):
-        self.all_of(self.near_in, back_out).wait_recv()
+        self.all_of(self.near_in.at[:back_count], back_out).wait_recv()
 
     def close(self):
         self.all_of(self.near_in, near_out).wait_send()
-        self.all_of(self.near_in, back_out).wait_send()
+        self.all_of(self.near_in.at[:back_count], back_out).wait_send()
+        for slot in range(len(relayed)):
+            self.all_of(self.near_in.at[0], relay_out + slot).wait_send()
 
         @pl.when(self.place.pair < half)
         def _():
@@ -410,6 +431,7 @@
     )
     sums[0].bridge(greeting)
     sums[0].gather()
+    sums[0].relay()
     sums[0].arrive()
 
     master[...] = stepped(master[...], total[...], step_scale(total))
@@ -420,14 +442,15 @@
     events = target_rows.shape[0]
     fresh = fresh_rows(stacked[0:events, :], target_rows[...], gru_input, gru_state)
     sums[1].exchange()
+    sums[0].close()
+    for hand in hands:
+        hand.wait_send()
     memory_out[...] = replaced(handed_memory, ids[3:4, :], fresh)
     sums[1].bridge(None)
     sums[1].gather()
+    sums[1].relay()
+    sums[1].close()
     sums[1].arrive()
-    for hand in hands:
-        hand.wait_send()
-    for each in sums:
-        each.close()
 
 
 def results_kernel(memory, master, total, logits, memory_out, decoder_out, logits_out, decoder, sems):
@@ -497,7 +520,7 @@
             vmem((hidden, width), bf16),
             dma((10,)),
             dma((2, 2)),
-            dma((batches, 2, 5)),
+            dma((batches, 2, relay_out + len(relayed))),
             pltpu.SemaphoreType.REGULAR,
         ],
         compiler_params=pltpu.CompilerParams(

time: 57 us -> 58.7 us (1.030)
  Pallas kernels: 56.3 us -> 57.9 us
    pallas_call x1, Pallas kernels: 55 us -> 56.6 us  [on_device(): pl.pallas_call(window_kernel, out_shape=(vmem((nodes, width), bf16), vmem...]
where the time goes in v10:
time: 58.7 us; the launch traced here: 58.5 us
  Pallas kernels  57.9 us (99%)
  between operations  0.64 us (1%)
    pallas_call x1, Pallas kernels, on_device(): pl.pallas_call(window_kernel, out_shape=(vmem((nodes, width), bf16), vmem...  56.6 us
    pallas_call x1, Pallas kernels, on_device(): pl.pallas_call(results_kernel, out_shape=(jax.ShapeDtypeStruct((1, nodes,...  1.27 us

profile of v10, /device:TPU:1, one launch (start us, length us, event | category | flops | bytes accessed | tf_op | source)
XLA Modules:
  0.0 58.5 jit_solution(18399076816910809056)
XLA Ops:
  0.6 56.6 %window.1 = (bf16[512,512]{1,0:T(8,128)(2,1)S(1)}, f32[256,512]{1,0:T(8,128)S(1)}, bf16[256,512]{1,0:T(8,128)(2,1)S(1)}, f32[4,256]{1,0:T(4,128)S(1)}) custom-call(bf16[512,512]{1,0:T(8,128)(2,1)} %memory_hbm.1, s32[10,512]{1,0:T(8,128)} %near_ids_hbm.1, s32[10,512]{1,0:T(8,128)} %near_times_hbm.1, s32[1,2,256]{2,1,0:T(2,128)} %source_ids_hbm.1, ...), custom_call_target="tpu_custom_call" | custom-call | tf_op jit(solution)/shard_map/window/pallas_call | solution.py:486
  57.2 1.3 %results.1 = (bf16[1,512,512]{2,1,0:T(8,128)(2,1)}, f32[1,512,256]{2,1,0:T(8,128)}, f32[1,4,256]{2,1,0:T(4,128)}) custom-call(bf16[512,512]{1,0:T(8,128)(2,1)S(1)} %get-tuple-element.7.memory, f32[256,512]{1,0:T(8,128)S(1)} %get-tuple-element.8.master, bf16[256,512]{1,0:T(8,128)(2,1)S(1)} %get-tuple-element.9.total, f32[4,256]{1,0:T(4,128)S(1)} %get-tuple-element.10.logits), custom_call_target="tpu_custom_call" | custom-call | tf_op jit(solution)/shard_map/results/pallas_call | solution.py:532

commit v11 on v8

--- a/solution.py
+++ b/solution.py
@@ -206,10 +206,9 @@
     stacked[events : 2 * events, :] = (0.5 * (rows + aggregate)).astype(bf16)
 
 
-def link_gradient(stacked, projection, logits, row, deltas, gradient, rounded):
+def link_gradient(stacked, projected, logits, row, deltas, gradient, rounded):
     events = stacked.shape[0] // 3
-    scale = 1.0 / projection.shape[0] ** 0.5
-    projected = matmul_nt(projection, stacked[...])
+    scale = 1.0 / projected.shape[0] ** 0.5
     source = projected[:, :events]
     target = projected[:, events : 2 * events]
     negative = projected[:, 2 * events :]
@@ -289,6 +288,7 @@
     picks,
     stacked,
     target_rows,
+    first_part,
     deltas,
     gradient,
     rounded,
@@ -352,9 +352,9 @@
         master[...] = decoder[...].astype(f32).T
 
     gather_events(memory, first_columns, table, count, picks, stacked, target_rows, loaded)
-    link_gradient(
-        stacked, master[...].astype(bf16), logits_out, 0, deltas, gradient, rounded.at[0]
-    )
+    start = master[...].astype(bf16)
+    projected = matmul_nt(start, stacked[...])
+    link_gradient(stacked, projected, logits_out, 0, deltas, gradient, rounded.at[0])
     pl.semaphore_wait(barrier, len(greeted) + half - 1 + half * (place.pair // half))
 
     @pl.when(place.pair >= half)
@@ -408,26 +408,27 @@
     gather_events(
         handed_memory, second_columns, table, count, picks, stacked, target_rows, lambda: None
     )
+    first_part[...] = matmul_nt(start, stacked[...])
     sums[0].bridge(greeting)
     sums[0].gather()
     sums[0].arrive()
 
-    master[...] = stepped(master[...], total[...], step_scale(total))
-    link_gradient(
-        stacked, master[...].astype(bf16), logits_out, 2, deltas, gradient, rounded.at[1]
-    )
+    scale = step_scale(total)
+    projected = first_part[...] - scale * matmul_nt(total[...], stacked[...])
+    link_gradient(stacked, projected, logits_out, 2, deltas, gradient, rounded.at[1])
     sums[1].scatter()
+    master[...] = stepped(master[...], total[...], scale)
     events = target_rows.shape[0]
     fresh = fresh_rows(stacked[0:events, :], target_rows[...], gru_input, gru_state)
     sums[1].exchange()
+    sums[0].close()
+    for hand in hands:
+        hand.wait_send()
     memory_out[...] = replaced(handed_memory, ids[3:4, :], fresh)
     sums[1].bridge(None)
     sums[1].gather()
+    sums[1].close()
     sums[1].arrive()
-    for hand in hands:
-        hand.wait_send()
-    for each in sums:
-        each.close()
 
 
 def results_kernel(memory, master, total, logits, memory_out, decoder_out, logits_out, decoder, sems):
@@ -488,6 +489,7 @@
             vmem((3 * events, nodes), bf16),
             vmem((3 * events, width), bf16),
             vmem((events, width), bf16),
+            vmem((hidden, 3 * events), f32),
             vmem((hidden, 3 * events), bf16),
             vmem((hidden, width), f32),
             vmem((batches, hidden, width), bf16),

time: 57 us -> 56.8 us (level)
  no operation moved by 1% of the time
where the time goes in v11:
time: 56.8 us; the launch traced here: 56.7 us
  Pallas kernels  56 us (99%)
  between operations  0.64 us (1%)
    pallas_call x1, Pallas kernels, on_device(): pl.pallas_call(window_kernel, out_shape=(vmem((nodes, width), bf16), vmem...  54.7 us
    pallas_call x1, Pallas kernels, on_device(): pl.pallas_call(results_kernel, out_shape=(jax.ShapeDtypeStruct((1, nodes,...  1.27 us

profile of v11, /device:TPU:1, one launch (start us, length us, event | category | flops | bytes accessed | tf_op | source)
XLA Modules:
  0.0 56.7 jit_solution(13187898800290361025)
XLA Ops:
  0.6 54.7 %window.1 = (bf16[512,512]{1,0:T(8,128)(2,1)S(1)}, f32[256,512]{1,0:T(8,128)S(1)}, bf16[256,512]{1,0:T(8,128)(2,1)S(1)}, f32[4,256]{1,0:T(4,128)S(1)}) custom-call(bf16[512,512]{1,0:T(8,128)(2,1)} %memory_hbm.1, s32[10,512]{1,0:T(8,128)} %near_ids_hbm.1, s32[10,512]{1,0:T(8,128)} %near_times_hbm.1, s32[1,2,256]{2,1,0:T(2,128)} %source_ids_hbm.1, ...), custom_call_target="tpu_custom_call" | custom-call | tf_op jit(solution)/shard_map/window/pallas_call | solution.py:464
  55.4 1.3 %results.1 = (bf16[1,512,512]{2,1,0:T(8,128)(2,1)}, f32[1,512,256]{2,1,0:T(8,128)}, f32[1,4,256]{2,1,0:T(4,128)}) custom-call(bf16[512,512]{1,0:T(8,128)(2,1)S(1)} %get-tuple-element.7.memory, f32[256,512]{1,0:T(8,128)S(1)} %get-tuple-element.8.master, bf16[256,512]{1,0:T(8,128)(2,1)S(1)} %get-tuple-element.9.total, f32[4,256]{1,0:T(4,128)S(1)} %get-tuple-element.10.logits), custom_call_target="tpu_custom_call" | custom-call | tf_op jit(solution)/shard_map/results/pallas_call | solution.py:511
